TPU v7x, 128 devices: a whole 4x4x4 slice. The times are simulated.
128 devices in a mesh: gx: 32 (over y, z, core), gy: 4 (over x).
Axes of the slice: x: 4, y: 4, z: 4, core: 2. Of those that a mesh axis runs over, the one named last changes fastest.
Arguments:
- features: bfloat16 [32, 256, 32, 128], P(None, 'gx', 'gy'), may hold values from -6 to 6
- w_enc1: bfloat16 [27, 32, 32], replicated, may hold values from -0.21875 to 0.21875
- w_enc2: bfloat16 [27, 64, 32], replicated, may hold values from -0.21875 to 0.21875
- w_enc3: bfloat16 [27, 128, 64], replicated, may hold values from -0.15625 to 0.15625
- w_enc4: bfloat16 [27, 256, 128], replicated, may hold values from -0.21875 to 0.21875
- w_dec3: bfloat16 [27, 128, 256], replicated, may hold values from -0.15625 to 0.15625
- w_dec2: bfloat16 [27, 64, 128], replicated, may hold values from -0.21875 to 0.21875
- w_dec1: bfloat16 [27, 32, 64], replicated, may hold values from -0.3125 to 0.3125
Outputs:
- decoded: bfloat16 [32, 256, 32, 128], P(None, 'gx', 'gy')
All inputs are finite; a program needn't handle non-finite values.
Results may differ from a plain program's by a relative error of at most 0.013.
Values may be sent and summed in bfloat16 or wider, within the bound.
A program may use at most 64 MiB of HBM per device.

v0:
```python
import functools

import jax
import jax.numpy as jnp
from jax import lax
from jax.experimental import pallas as pl
from jax.experimental.pallas import tpu as pltpu
from jax.sharding import PartitionSpec as P

BF = jnp.bfloat16
F32 = jnp.float32
MESH = pl.DeviceIdType.MESH
DIRS = [(dx, dy) for dx in (-1, 0, 1) for dy in (-1, 0, 1) if (dx, dy) != (0, 0)]
TAPS = (((0,), (1, 2)), ((0, 1), (2,)))


def nn(a, b):
    return lax.dot_general(a, b, (((1,), (0,)), ((), ())), preferred_element_type=F32)


def nt(a, b):
    return lax.dot_general(a, b, (((1,), (1,)), ((), ())), preferred_element_type=F32)


def iota(shape, dim):
    return lax.broadcasted_iota(jnp.int32, shape, dim)


def ones_where(mask):
    return jnp.where(mask, 1.0, 0.0).astype(BF)


def gelu(x):
    return 0.5 * x * (1.0 + jnp.tanh(0.7978845608028654 * (x + 0.044715 * (x * x * x))))


def shifted(v, step, axis, period):
    n = v.shape[axis]
    place = iota(v.shape, axis) % period
    edge = 0 if step == 1 else period - 1
    return jnp.where(place == edge, 0.0, pltpu.roll(v, step % n, axis))


def cat(parts, axis):
    return parts[0] if len(parts) == 1 else jnp.concatenate(parts, axis=axis)


def side(d, n, width=1, pad=1):
    if d == 1:
        return (pad + (n - 1)) * width, 0, width
    if d == -1:
        return pad * width, (n + pad) * width, width
    return pad * width, pad * width, n * width


def kernel(
    feat, w1h, w2h, w3h, w4h, v3h, v2h, v1h, out,
    fv, w1, w2, w3, w4, v3, v2, v1, ov,
    fext, e1, pbs, p1, y1s, y1r, p2, y2s, y2r, p3, e2e, e3e,
    k1, k2, k3, g2, g1, pd3, d3e, d2e, q, dd,
    lsem, osem, s1, r1, s2, r2, s3, r3, s4, r4, se2, re2, se3, re3,
):
    gx, gy = lax.axis_index("gx"), lax.axis_index("gy")
    nx, ny = lax.axis_size("gx"), lax.axis_size("gy")

    loads = [
        pltpu.make_async_copy(src, dst, lsem.at[n])
        for n, (src, dst) in enumerate(
            [(feat, fv), (w1h, w1), (w2h, w2), (w3h, w3), (w4h, w4), (v3h, v3), (v2h, v2), (v1h, v1)]
        )
    ]
    for c in loads:
        c.start()

    def target(dx, dy):
        return (lax.rem(gx + dx + nx, nx), lax.rem(gy + dy + ny, ny))

    window = [(dx, dy) for dx in range(-2, 3) for dy in range(ny) if (dx, dy) != (0, 0)]
    barrier = pltpu.get_barrier_semaphore()
    for dx, dy in window:
        pl.semaphore_signal(barrier, inc=1, device_id=target(dx, dy), device_id_type=MESH)

    def send(n, dx, dy, src, dst, ss, rs):
        return pltpu.make_async_remote_copy(
            src_ref=src, dst_ref=dst, send_sem=ss.at[n], recv_sem=rs.at[n],
            device_id=target(dx, dy), device_id_type=MESH,
        )

    def start(copies):
        for c in copies:
            c.start()

    def arrive(copies):
        for c in copies:
            c.wait_recv()

    loads[0].wait()
    r, c = iota((256, 256), 0), iota((256, 256), 1)
    perm = ones_where((r // 32 == c % 8) & (r % 32 == c // 8))
    perm_t = ones_where((c // 32 == r % 8) & (c % 32 == r // 8))

    def place(x, carry):
        a = fv[:, pl.ds(2 * x, 1)].astype(F32).reshape(256, 128).astype(BF)
        b = fv[:, pl.ds(2 * x + 1, 1)].astype(F32).reshape(256, 128).astype(BF)
        t = nn(perm, cat([a, b], 1)).astype(BF)
        fext[2 * x + 1, pl.ds(32, 256), :] = t[:, :128]
        fext[2 * x + 2, pl.ds(32, 256), :] = t[:, 128:]
        return carry

    lax.fori_loop(0, 4, place, 0)
    for n in range(4):
        p3[:, n if n < 2 else n + 4] = jnp.zeros((5, 16, 128), BF)
    pl.semaphore_wait(barrier, len(window))

    x1 = []
    for n, (dx, dy) in enumerate(DIRS):
        sx, tx, cx = side(dx, 8)
        sy, ty, cy = side(dy, 8, 32)
        x1.append(
            send(n, dx, dy, fext.at[pl.ds(sx, cx), pl.ds(sy, cy)], fext.at[pl.ds(tx, cx), pl.ds(ty, cy)], s1, r1)
        )
    start(x1)

    loads[1].wait()
    z32 = jnp.zeros((32, 32), BF)
    for l in range(3):
        for yo in range(2):
            row = []
            for i in range(3):
                for yi in range(4):
                    j = yi - yo
                    row.append(w1[9 * i + 3 * j + l] if 0 <= j < 3 else z32)
            k1[pl.ds(64 * l + 32 * yo, 32), :] = cat(row, 1)
    loads[2].wait()
    z64 = jnp.zeros((64, 32), BF)
    for l in range(3):
        for yo in range(4):
            row = []
            for i in range(3):
                for yi in (0, 1, 2, 3, -1, 4, 9, 9):
                    j = yi - yo + 1
                    row.append(w2[9 * i + 3 * j + l] if 0 <= j < 3 else z64)
            k2[pl.ds(256 * l + 64 * yo, 64), :] = cat(row, 1)
    loads[3].wait()
    z128 = jnp.zeros((128, 64), BF)
    for l in range(3):
        for yo in range(2):
            row = []
            for i in range(3):
                for yi in (0, 1, -1, 2):
                    j = yi - yo + 1
                    row.append(w3[9 * i + 3 * j + l] if 0 <= j < 3 else z128)
            k3[pl.ds(256 * l + 128 * yo, 128), :] = cat(row, 1)

    arrive(x1)

    @pl.when(gx == 0)
    def _():
        fext[0] = jnp.zeros((320, 128), BF)

    @pl.when(gx == nx - 1)
    def _():
        fext[9] = jnp.zeros((320, 128), BF)

    @pl.when(gy == 0)
    def _():
        fext[:, pl.ds(0, 32)] = jnp.zeros((10, 32, 128), BF)

    @pl.when(gy == ny - 1)
    def _():
        fext[:, pl.ds(288, 32)] = jnp.zeros((10, 32, 128), BF)

    def enc1(x, carry):
        for b in range(4):
            rhs = cat(
                [
                    cat([fext[2 * x + i, pl.ds(64 * b, 128), :], fext[2 * x + 1 + i, pl.ds(64 * b, 128), :]], 1)
                    for i in range(3)
                ],
                0,
            )
            t = nn(k1[...], rhs)
            total = None
            for h in range(2):
                u = t[:, 128 * h : 128 * (h + 1)]
                v = u[64:128] + shifted(u[:64], 1, 1, 128) + shifted(u[128:], -1, 1, 128)
                v = gelu(v).astype(BF)
                e1[2 * x + h, pl.ds(64 * b, 64), :] = v
                f = v.astype(F32)
                f = f[:32] + f[32:]
                total = f if total is None else total + f
            total = total + pltpu.roll(total, 127, 1)
            pbs[x, pl.ds(32 * b, 32), :] = (total * 0.125).astype(BF)
        return carry

    lax.fori_loop(0, 4, enc1, 0)

    pick64 = ones_where(iota((64, 128), 1) == 2 * iota((64, 128), 0))
    for s, y in ((0, 0), (1, 96)):
        y1s[s] = nt(pick64, cat([pbs[x, pl.ds(y, 32), :] for x in range(4)], 0)).astype(BF)
    for x in range(4):
        p1[x + 1] = nt(pick64, pbs[x]).astype(BF)

    def halo(main, ys, yr, n_local, ss, rs):
        copies = []
        for n, (dx, dy) in enumerate(DIRS):
            if dy == 0:
                sx, tx, _ = side(dx, n_local)
                copies.append(send(n, dx, dy, main.at[sx], main.at[tx], ss, rs))
            else:
                s = 1 if dy == 1 else 0
                copies.append(send(n, dx, dy, ys.at[s], yr.at[1 - s, 1 - dx], ss, rs))
        return copies

    x2 = halo(p1, y1s, y1r, 4, s2, r2)
    start(x2)
    arrive(x2)

    def sides(yr, n_local, c):
        found = []
        for x in range(n_local + 2):
            slot, at = (0, n_local - 1) if x == 0 else (2, 0) if x == n_local + 1 else (1, x - 1)
            inside = (gx > 0) if x == 0 else (gx < nx - 1) if x == n_local + 1 else True
            lo = yr[0, slot][:, at * c : (at + 1) * c]
            hi = yr[1, slot][:, at * c : (at + 1) * c]
            zero = jnp.zeros_like(lo)
            lo = jnp.where(inside & (gy > 0), lo, zero)
            hi = jnp.where(inside & (gy < ny - 1), hi, zero)
            parts = [lo, hi]
            if c < 64:
                parts.append(jnp.zeros((lo.shape[0], 128 - 2 * c), BF))
            found.append(cat(parts, 1))
        return found

    def mains(main, n_local):
        found = []
        for x in range(n_local + 2):
            v = main[x]
            if x == 0:
                v = jnp.where(gx > 0, v, jnp.zeros_like(v))
            if x == n_local + 1:
                v = jnp.where(gx < nx - 1, v, jnp.zeros_like(v))
            found.append(v)
        return found

    m1, h1 = mains(p1, 4), sides(y1r, 4, 32)
    lhs = cat([cat([cat([m1[x + i], h1[x + i]], 1) for i in range(3)], 1) for x in range(4)], 0)
    t = nt(lhs, k2[...])
    e2 = gelu(t[:, 256:512] + shifted(t[:, :256], 1, 0, 64) + shifted(t[:, 512:], -1, 0, 64)).astype(BF)
    f = e2.astype(F32)
    low = iota((64, 128), 1) < 64
    pick32 = ones_where(iota((32, 64), 1) == 2 * iota((32, 64), 0))
    p2v = []
    for x in range(2):
        a = f[128 * x : 128 * x + 64] + f[128 * x + 64 : 128 * x + 128]
        a0, a1 = a[:, :128], a[:, 128:]
        a = jnp.where(low, a0 + pltpu.roll(a0, 64, 1), a1 + pltpu.roll(a1, 64, 1))
        a = (a + pltpu.roll(a, 63, 0)) * 0.125
        a = nn(pick32, a.astype(BF))
        p2v.append(a)
        p2[x + 1] = a.astype(BF)
    low32 = iota((32, 128), 1) < 64
    y2s[0] = jnp.where(low32, p2v[0], pltpu.roll(p2v[1], 64, 1)).astype(BF)
    y2s[1] = jnp.where(low32, pltpu.roll(p2v[0], 64, 1), p2v[1]).astype(BF)
    x3 = halo(p2, y2s, y2r, 2, s3, r3)
    start(x3)

    rr, cc = iota((64, 64), 0), iota((64, 64), 1)
    split = ones_where(cc == 2 * (rr % 32) + rr // 32)
    for x in range(4):
        a = nn(split, e2[64 * x : 64 * x + 64])
        for y in range(4):
            ev = a[:32, 128 * (y // 2) : 128 * (y // 2) + 128]
            od = a[32:, 128 * (y // 2) : 128 * (y // 2) + 128]
            if y % 2 == 0:
                cell = jnp.where(low32, ev, pltpu.roll(od, 64, 1))
            else:
                cell = jnp.where(low32, pltpu.roll(ev, 64, 1), od)
            e2e[x + 1, y + 1] = cell.astype(BF)

    def cells(ref, n_local, ss, rs):
        copies = []
        for n, (dx, dy) in enumerate(DIRS):
            sx, tx, cx = side(dx, n_local)
            sy, ty, cy = side(dy, n_local)
            copies.append(
                send(n, dx, dy, ref.at[pl.ds(sx, cx), pl.ds(sy, cy)], ref.at[pl.ds(tx, cx), pl.ds(ty, cy)], ss, rs)
            )
        return copies

    xe2 = cells(e2e, 4, se2, re2)
    start(xe2)
    arrive(x3)

    m2, h2 = mains(p2, 2), sides(y2r, 2, 64)
    lhs = cat([cat([cat([m2[x + i], h2[x + i]], 1) for i in range(3)], 1) for x in range(2)], 0)
    t = nt(lhs, k3[...])
    e3 = gelu(t[:, 256:512] + shifted(t[:, :256], 1, 0, 32) + shifted(t[:, 512:], -1, 0, 32)).astype(BF)
    f = e3.astype(F32)
    a = f[:32] + f[32:]
    a = a[:, :128] + a[:, 128:]
    a = (a + pltpu.roll(a, 31, 0)) * 0.125
    pick16 = ones_where(iota((16, 32), 1) == 2 * iota((16, 32), 0))
    p3[2, gy + 2] = nn(pick16, a.astype(BF)).astype(BF)
    x4 = []
    for n, (dx, dy) in enumerate(window):
        x4.append(send(n, dx, dy, p3.at[2, gy + 2], p3.at[2 - dx, gy + 2], s4, r4))
    start(x4)
    for x in range(2):
        for y in range(2):
            e3e[x + 1, y + 1] = e3[32 * x : 32 * x + 32, 128 * y : 128 * y + 128]
    xe3 = cells(e3e, 2, se3, re3)
    start(xe3)

    loads[6].wait()
    for px in range(2):
        for py in range(2):
            for tx in range(2):
                for ty in range(2):
                    s = []
                    for l in range(3):
                        terms = [
                            v2[9 * i + 3 * j + l].astype(F32) for i in TAPS[px][tx] for j in TAPS[py][ty]
                        ]
                        s.append(functools.reduce(jnp.add, terms))
                    block = cat([s[0], s[2], s[1] + s[2], s[0] + s[1]], 0).astype(BF)
                    g2[pl.ds(256 * (2 * px + py), 256), pl.ds(128 * (2 * tx + ty), 128)] = block
    loads[7].wait()
    for px in range(2):
        for py in range(2):
            for l in range(3):
                row = []
                for tx in range(2):
                    for ty in range(2):
                        terms = [
                            v1[9 * i + 3 * j + l].astype(F32) for i in TAPS[px][tx] for j in TAPS[py][ty]
                        ]
                        row.append(functools.reduce(jnp.add, terms).astype(BF))
                g1[pl.ds(96 * (2 * px + py) + 32 * l, 32), :] = cat(row, 1)

    loads[4].wait()
    for n, (dx, dy) in enumerate(window):
        pltpu.make_async_remote_copy(
            src_ref=p3.at[2, gy + 2], dst_ref=p3.at[2 - dx, lax.rem(gy - dy + ny, ny) + 2],
            send_sem=s4.at[n], recv_sem=r4.at[n], device_id=target(dx, dy), device_id_type=MESH,
        ).wait_recv()

    cell = []
    for x in range(5):
        inside = (gx + (x - 2) >= 0) & (gx + (x - 2) < nx)
        line = []
        for y in range(5):
            v = p3[x, gy + y]
            line.append(jnp.where(inside, v, jnp.zeros_like(v)))
        cell.append(line)
    lhs = cat(
        [
            cat([cell[x + i][y + j] for i in range(3) for j in range(3)], 1)
            for x in range(3)
            for y in range(3)
        ],
        0,
    )
    t = cat(
        [nt(lhs, cat([w4[9 * i + 3 * j + l] for i in range(3) for j in range(3)], 1)) for l in range(3)], 1
    )
    e4 = gelu(t[:, 256:512] + shifted(t[:, :256], 1, 0, 16) + shifted(t[:, 512:], -1, 0, 16))

    def inside(x, y, width, n_local):
        ok = True
        if x == 0:
            ok = gx > 0
        if x == n_local + 1:
            ok = gx < nx - 1
        if y == 0:
            ok = ok & (gy > 0)
        if y == n_local + 1:
            ok = ok & (gy < ny - 1)
        return ok

    def kept(v, ok):
        return v if ok is True else jnp.where(ok, v, jnp.zeros_like(v))

    e4 = [kept(e4[16 * n : 16 * n + 16], inside(n // 3, n % 3, 16, 1)).astype(BF) for n in range(9)]

    loads[5].wait()
    twice = ones_where(iota((32, 16), 1) == iota((32, 16), 0) // 2)
    up = nn(twice, cat(e4, 1)).astype(BF)
    at = ((0, 0, 1), (0, 1, 1), (1, 1, 2), (1, 2, 2))
    for x in range(4):
        for y in range(4):
            for i in range(3):
                for j in range(3):
                    n = 3 * at[x][i] + at[y][j]
                    pd3[pl.ds(128 * x + 32 * y, 32), pl.ds(256 * (3 * i + j), 256)] = up[:, 256 * n : 256 * n + 256]
    arrive(xe3)
    for x in range(4):
        t = None
        for i in range(3):
            for j in range(3):
                u = nt(
                    pd3[pl.ds(128 * x, 128), pl.ds(256 * (3 * i + j), 256)],
                    cat([v3[9 * i + 3 * j + l] for l in range(3)], 0),
                )
                t = u if t is None else t + u
        v = gelu(t[:, 128:256] + shifted(t[:, :128], 1, 0, 32) + shifted(t[:, 256:], -1, 0, 32))
        for y in range(4):
            w = v[32 * y : 32 * y + 32] + e3e[x, y].astype(F32)
            d3e[x, y] = kept(w, inside(x, y, 32, 2)).astype(BF)

    arrive(xe2)
    lane96 = iota((96, 128), 1) < 64
    for k in range(3):
        lhs = cat(
            [cat([d3e[k, m], d3e[k, m + 1], d3e[k + 1, m], d3e[k + 1, m + 1]], 1) for m in range(3)], 0
        )
        t = nt(lhs, g2[...])
        for px in range(2):
            for py in range(2):
                n = 256 * (2 * px + py)
                a, b = t[:, n : n + 128], t[:, n + 128 : n + 256]
                v = gelu(b + jnp.where(lane96, shifted(a, 1, 0, 32), shifted(a, -1, 0, 32)))
                for m in range(3):
                    x, y = 2 * k + 1 - px, 2 * m + 1 - py
                    w = v[32 * m : 32 * m + 32] + e2e[x, y].astype(F32)
                    d2e[x, y] = kept(w, inside(x, y, 32, 4))

    rr, cc = iota((128, 64), 0), iota((128, 64), 1)
    spread = ones_where((rr // 4 == cc % 32) & (rr // 2 % 2 == cc // 32))
    for x in range(6):
        line = []
        for m in range(5):
            a, b = d2e[x, m], d2e[x, m + 1]
            top = jnp.where(low32, a, pltpu.roll(b, 64, 1))
            bottom = jnp.where(low32, pltpu.roll(a, 64, 1), b)
            line.append(cat([top, bottom], 0).astype(BF))
        a = nn(spread, cat(line, 1)).astype(BF)
        for m in range(5):
            q[x, m] = a[:, 128 * m : 128 * m + 128]

    for k in range(5):
        for m in range(5):
            t = nt(g1[...], cat([q[k, m], q[k + 1, m]], 1))
            for px in range(2):
                for py in range(2):
                    a, b = k - px, m - py
                    if not (0 <= a < 4 and 0 <= b < 4):
                        continue
                    x, y = 2 * a + px, 2 * b + py
                    u = t[96 * (2 * px + py) : 96 * (2 * px + py) + 96]
                    v = gelu(u[32:64] + shifted(u[:32], 1, 1, 128) + shifted(u[64:], -1, 1, 128))
                    v = v + e1[x, pl.ds(32 * y, 32), :].astype(F32)
                    dd[x, pl.ds(32 * y, 32), :] = v.astype(BF)

    def back(x, carry):
        t = nn(perm_t, cat([dd[2 * x], dd[2 * x + 1]], 1))
        for h in range(2):
            u = t[:, 128 * h : 128 * h + 128].reshape(32, 1, 8, 128).astype(BF)
            ov[:, pl.ds(2 * x + h, 1)] = u
        return carry

    lax.fori_loop(0, 4, back, 0)
    done = pltpu.make_async_copy(ov, out, osem)
    done.start()
    for copies in (x1, x2, x3, x4, xe2, xe3):
        for c in copies:
            c.wait_send()
    done.wait()


def local(features, w_enc1, w_enc2, w_enc3, w_enc4, w_dec3, w_dec2, w_dec1):
    args = (features, w_enc1, w_enc2, w_enc3, w_enc4, w_dec3, w_dec2, w_dec1)
    ny = lax.axis_size("gy")
    far = 5 * ny - 1
    dma = pltpu.SemaphoreType.DMA
    scratch = [pltpu.VMEM(a.shape, BF) for a in args]
    scratch.append(pltpu.VMEM((32, 8, 8, 128), BF))
    for shape in (
        (10, 320, 128), (8, 256, 128), (4, 128, 128),
        (6, 64, 128), (2, 64, 128), (2, 3, 64, 128),
        (4, 32, 128), (2, 32, 128), (2, 3, 32, 128),
        (5, ny + 4, 16, 128), (6, 6, 32, 128), (4, 4, 32, 128),
        (192, 384), (768, 768), (768, 768), (1024, 512), (384, 256),
        (512, 2304), (4, 4, 32, 128),
    ):
        scratch.append(pltpu.VMEM(shape, BF))
    scratch.append(pltpu.VMEM((6, 6, 32, 128), F32))
    scratch.append(pltpu.VMEM((6, 5, 128, 128), BF))
    scratch.append(pltpu.VMEM((8, 256, 128), BF))
    scratch += [dma((8,)), dma]
    for n in (8, 8, 8, far, 8, 8):
        scratch += [dma((n,)), dma((n,))]
    return pl.pallas_call(
        kernel,
        out_shape=jax.ShapeDtypeStruct(features.shape, BF),
        in_specs=[pl.BlockSpec(memory_space=pl.ANY)] * 8,
        out_specs=pl.BlockSpec(memory_space=pl.ANY),
        scratch_shapes=scratch,
        compiler_params=pltpu.CompilerParams(
            collective_id=0, has_side_effects=True, vmem_limit_bytes=56 * 1024 * 1024
        ),
        cost_estimate=pl.CostEstimate(flops=2 * 1115000000, bytes_accessed=7000000, transcendentals=1000000),
    )(*args)


def solution(mesh):
    return jax.shard_map(
        local,
        mesh=mesh,
        in_specs=(P(None, "gx", "gy", None), P(), P(), P(), P(), P(), P(), P()),
        out_specs=P(None, "gx", "gy", None),
        check_vma=False,
    )
```

profile of v0, /device:TPU:1, one launch (start us, length us, event | category | flops | bytes accessed | tf_op | source)
XLA Modules:
  0.0 49.7 jit_solution(17858221200395471370)
XLA Ops:
  0.0 1.9 %copy.9.w2h = bf16[27,64,32]{2,1,0:T(8,128)(2,1)} copy(bf16[27,64,32]{1,2,0:T(8,128)(2,1)} %param.10) | data formatting | bytes 221184 | tf_op args[2]
  1.9 2.2 %copy.10.w3h = bf16[27,128,64]{2,1,0:T(8,128)(2,1)} copy(bf16[27,128,64]{1,2,0:T(8,128)(2,1)} %param.11) | data formatting | bytes 884736 | tf_op args[3]
  4.1 43.7 %shard_map.82 = bf16[32,8,8,128]{3,2,1,0:T(8,128)(2,1)} custom-call(bf16[32,8,8,128]{3,2,1,0:T(8,128)(2,1)} %feat.1, bf16[27,32,32]{2,1,0:T(8,128)(2,1)} %w1h.1, bf16[27,64,32]{2,1,0:T(8,128)(2,1)} %copy.9.w2h, bf16[27,128,64]{2,1,0:T(8,128)(2,1)} %copy.10.w3h, bf16[27,256,128]{2,1,0:T(8,128)(2,1)} %w4h.1, bf16[27,128,256]{2,1,0:T(8,128)(2,1)} %v3h.1, ...), custom_call_target="tpu_custom_call" | custom-call | flops 2230000128 | bytes 7000000 | tf_op jit(solution)/shard_map/pallas_call | solution.py:493
  47.8 1.9 %copy.12 = bf16[32,8,8,128]{3,2,1,0:T(8,128)(2,1)} copy(bf16[32,8,8,128]{3,2,1,0:T(8,128)(2,1)} %shard_map.82) | data formatting | bytes 1048576
where the time goes:
time: 49.9 us; the launch traced here: 49.7 us
  Pallas kernels  43.7 us (88%)
  local copies, waits for them, and re-layouts  6.01 us (12%)
    pallas_call x1, Pallas kernels, local(): pl.pallas_call(kernel, out_shape=jax.ShapeDtypeStruct(features.shape, BF)...  43.7 us
    unnamed x3, local copies, waits for them, and re-layouts  6.01 us

commit v1 on v0

--- a/solution.py
+++ b/solution.py
@@ -132,25 +132,25 @@
                     row.append(w1[9 * i + 3 * j + l] if 0 <= j < 3 else z32)
             k1[pl.ds(64 * l + 32 * yo, 32), :] = cat(row, 1)
     loads[2].wait()
-    z64 = jnp.zeros((64, 32), BF)
-    for l in range(3):
-        for yo in range(4):
+    z64 = jnp.zeros((32, 64), BF)
+    for i in range(3):
+        for n, yi in enumerate((0, 1, 2, 3, -1, 4, 9, 9)):
             row = []
-            for i in range(3):
-                for yi in (0, 1, 2, 3, -1, 4, 9, 9):
+            for l in range(3):
+                for yo in range(4):
                     j = yi - yo + 1
                     row.append(w2[9 * i + 3 * j + l] if 0 <= j < 3 else z64)
-            k2[pl.ds(256 * l + 64 * yo, 64), :] = cat(row, 1)
+            k2[pl.ds(256 * i + 32 * n, 32), :] = cat(row, 1)
     loads[3].wait()
-    z128 = jnp.zeros((128, 64), BF)
-    for l in range(3):
-        for yo in range(2):
-            row = []
-            for i in range(3):
-                for yi in (0, 1, -1, 2):
+    z128 = jnp.zeros((64, 128), BF)
+    for i in range(3):
+        for n, yi in enumerate((0, 1, -1, 2)):
+            for l in range(3):
+                for yo in range(2):
                     j = yi - yo + 1
-                    row.append(w3[9 * i + 3 * j + l] if 0 <= j < 3 else z128)
-            k3[pl.ds(256 * l + 128 * yo, 128), :] = cat(row, 1)
+                    k3[pl.ds(256 * i + 64 * n, 64), pl.ds(256 * l + 128 * yo, 128)] = (
+                        w3[9 * i + 3 * j + l] if 0 <= j < 3 else z128
+                    )
 
     arrive(x1)
 
@@ -245,7 +245,7 @@
 
     m1, h1 = mains(p1, 4), sides(y1r, 4, 32)
     lhs = cat([cat([cat([m1[x + i], h1[x + i]], 1) for i in range(3)], 1) for x in range(4)], 0)
-    t = nt(lhs, k2[...])
+    t = nn(lhs, k2[...])
     e2 = gelu(t[:, 256:512] + shifted(t[:, :256], 1, 0, 64) + shifted(t[:, 512:], -1, 0, 64)).astype(BF)
     f = e2.astype(F32)
     low = iota((64, 128), 1) < 64
@@ -294,7 +294,7 @@
 
     m2, h2 = mains(p2, 2), sides(y2r, 2, 64)
     lhs = cat([cat([cat([m2[x + i], h2[x + i]], 1) for i in range(3)], 1) for x in range(2)], 0)
-    t = nt(lhs, k3[...])
+    t = nn(lhs, k3[...])
     e3 = gelu(t[:, 256:512] + shifted(t[:, :256], 1, 0, 32) + shifted(t[:, 512:], -1, 0, 32)).astype(BF)
     f = e3.astype(F32)
     a = f[:32] + f[32:]
@@ -469,6 +469,7 @@
 
 
 def local(features, w_enc1, w_enc2, w_enc3, w_enc4, w_dec3, w_dec2, w_dec1):
+    w_enc2, w_enc3 = jnp.swapaxes(w_enc2, 1, 2), jnp.swapaxes(w_enc3, 1, 2)
     args = (features, w_enc1, w_enc2, w_enc3, w_enc4, w_dec3, w_dec2, w_dec1)
     ny = lax.axis_size("gy")
     far = 5 * ny - 1

time: 49.9 us -> 45.7 us (0.916)
  local copies, waits for them, and re-layouts: 6.01 us -> 1.87 us
    unnamed x3 -> x1, local copies, waits for them, and re-layouts: 6.01 us -> 1.87 us
where the time goes in v1:
time: 45.7 us; the launch traced here: 45.6 us
  Pallas kernels  43.7 us (96%)
  local copies, waits for them, and re-layouts  1.87 us (4%)
    pallas_call x1, Pallas kernels, local(): pl.pallas_call(kernel, out_shape=jax.ShapeDtypeStruct(features.shape, BF)...  43.7 us
    unnamed x1, local copies, waits for them, and re-layouts  1.87 us

profile of v1, /device:TPU:1, one launch (start us, length us, event | category | flops | bytes accessed | tf_op | source)
XLA Modules:
  0.0 45.6 jit_solution(14045004572054747007)
XLA Ops:
  0.0 43.7 %shard_map.82 = bf16[32,8,8,128]{3,2,1,0:T(8,128)(2,1)} custom-call(bf16[32,8,8,128]{3,2,1,0:T(8,128)(2,1)} %feat.1, bf16[27,32,32]{2,1,0:T(8,128)(2,1)} %w1h.1, bf16[27,32,64]{2,1,0:T(8,128)(2,1)} %bitcast.3, bf16[27,64,128]{2,1,0:T(8,128)(2,1)} %bitcast.2, bf16[27,256,128]{2,1,0:T(8,128)(2,1)} %w4h.1, bf16[27,128,256]{2,1,0:T(8,128)(2,1)} %v3h.1, ...), custom_call_target="tpu_custom_call" | custom-call | flops 2230000128 | bytes 7000000 | tf_op jit(solution)/shard_map/pallas_call | solution.py:494
  43.7 1.9 %copy.10 = bf16[32,8,8,128]{3,2,1,0:T(8,128)(2,1)} copy(bf16[32,8,8,128]{3,2,1,0:T(8,128)(2,1)} %shard_map.82) | data formatting | bytes 1048576

commit v2 on v1

--- a/solution.py
+++ b/solution.py
@@ -10,7 +10,7 @@
 BF = jnp.bfloat16
 F32 = jnp.float32
 MESH = pl.DeviceIdType.MESH
-DIRS = [(dx, dy) for dx in (-1, 0, 1) for dy in (-1, 0, 1) if (dx, dy) != (0, 0)]
+DIRS = [(-1, -1), (-1, 1), (1, -1), (1, 1), (-1, 0), (1, 0), (0, -1), (0, 1)]
 TAPS = (((0,), (1, 2)), ((0, 1), (2,)))
 
 
@@ -55,30 +55,39 @@
 
 def kernel(
     feat, w1h, w2h, w3h, w4h, v3h, v2h, v1h, out,
-    fv, w1, w2, w3, w4, v3, v2, v1, ov,
-    fext, e1, pbs, p1, y1s, y1r, p2, y2s, y2r, p3, e2e, e3e,
-    k1, k2, k3, g2, g1, pd3, d3e, d2e, q, dd,
+    fv, w1, w2, w3, v2, v1,
+    fext, e1, p1, y1s, y1r, p2, y2s, y2r, p3, e2e, e3e,
+    k1, k2, k3, k4, kd3, g2, g1, pd3, d3e, d2e, q, dd,
     lsem, osem, s1, r1, s2, r2, s3, r3, s4, r4, se2, re2, se3, re3,
 ):
     gx, gy = lax.axis_index("gx"), lax.axis_index("gy")
     nx, ny = lax.axis_size("gx"), lax.axis_size("gy")
 
-    loads = [
-        pltpu.make_async_copy(src, dst, lsem.at[n])
-        for n, (src, dst) in enumerate(
-            [(feat, fv), (w1h, w1), (w2h, w2), (w3h, w3), (w4h, w4), (v3h, v3), (v2h, v2), (v1h, v1)]
-        )
-    ]
-    for c in loads:
+    loads = []
+
+    def load(src, dst):
+        c = pltpu.make_async_copy(src, dst, lsem.at[len(loads)])
         c.start()
+        loads.append(c)
+        return c
 
     def target(dx, dy):
         return (lax.rem(gx + dx + nx, nx), lax.rem(gy + dy + ny, ny))
 
+    barrier = pltpu.get_barrier_semaphore()
+    got_feat = load(feat, fv)
+    for dx, dy in DIRS:
+        pl.semaphore_signal(barrier, inc=1, device_id=target(dx, dy), device_id_type=MESH)
+    got_w1, got_w2, got_w3 = load(w1h, w1), load(w2h, w2), load(w3h, w3)
+    got_v2, got_v1 = load(v2h, v2), load(v1h, v1)
+    got_w4 = [load(w4h.at[n], k4.at[:, pl.ds(128 * n, 128)]) for n in range(9)]
+    got_v3 = [load(v3h.at[n], kd3.at[:, pl.ds(256 * n, 256)]) for n in range(9)]
+
+    def far(d):
+        return abs(d[0]) + min(d[1], ny - d[1])
+
     window = [(dx, dy) for dx in range(-2, 3) for dy in range(ny) if (dx, dy) != (0, 0)]
-    barrier = pltpu.get_barrier_semaphore()
-    for dx, dy in window:
-        pl.semaphore_signal(barrier, inc=1, device_id=target(dx, dy), device_id_type=MESH)
+    window.sort(key=far, reverse=True)
 
     def send(n, dx, dy, src, dst, ss, rs):
         return pltpu.make_async_remote_copy(
@@ -94,10 +103,9 @@
         for c in copies:
             c.wait_recv()
 
-    loads[0].wait()
+    got_feat.wait()
     r, c = iota((256, 256), 0), iota((256, 256), 1)
     perm = ones_where((r // 32 == c % 8) & (r % 32 == c // 8))
-    perm_t = ones_where((c // 32 == r % 8) & (c % 32 == r // 8))
 
     def place(x, carry):
         a = fv[:, pl.ds(2 * x, 1)].astype(F32).reshape(256, 128).astype(BF)
@@ -110,7 +118,7 @@
     lax.fori_loop(0, 4, place, 0)
     for n in range(4):
         p3[:, n if n < 2 else n + 4] = jnp.zeros((5, 16, 128), BF)
-    pl.semaphore_wait(barrier, len(window))
+    pl.semaphore_wait(barrier, len(DIRS))
 
     x1 = []
     for n, (dx, dy) in enumerate(DIRS):
@@ -121,27 +129,56 @@
         )
     start(x1)
 
-    loads[1].wait()
-    z32 = jnp.zeros((32, 32), BF)
-    for l in range(3):
-        for yo in range(2):
-            row = []
-            for i in range(3):
-                for yi in range(4):
-                    j = yi - yo
-                    row.append(w1[9 * i + 3 * j + l] if 0 <= j < 3 else z32)
-            k1[pl.ds(64 * l + 32 * yo, 32), :] = cat(row, 1)
-    loads[2].wait()
-    z64 = jnp.zeros((32, 64), BF)
+    got_w1.wait()
+    t = None
+    r, c = iota((32, 256), 0), iota((32, 256), 1)
+    for j in range(3):
+        taps = cat([w1[pl.ds(9 * i + 3 * j, 3)].reshape(96, 32) for i in range(3)], 0)
+        u = nn(taps, ones_where((r == c % 32) & (c // 32 % 4 == c // 128 + j)))
+        t = u if t is None else t + u
+    t = t.astype(BF)
     for i in range(3):
-        for n, yi in enumerate((0, 1, 2, 3, -1, 4, 9, 9)):
-            row = []
+        for l in range(3):
+            for yo in range(2):
+                k1[pl.ds(64 * l + 32 * yo, 32), pl.ds(128 * i, 128)] = t[
+                    96 * i + 32 * l : 96 * i + 32 * l + 32, 128 * yo : 128 * yo + 128
+                ]
+
+    def enc1(xa, xb, b):
+        rhs = cat(
+            [cat([fext[xa + i, pl.ds(64 * b, 128), :], fext[xb + i, pl.ds(64 * b, 128), :]], 1) for i in range(3)],
+            0,
+        )
+        t = nn(k1[...], rhs)
+        for h, x in enumerate((xa, xb)):
+            u = t[:, 128 * h : 128 * (h + 1)]
+            v = u[64:128] + shifted(u[:64], 1, 1, 128) + shifted(u[128:], -1, 1, 128)
+            e1[x, pl.ds(64 * b, 64), :] = gelu(v).astype(BF)
+
+    def enc1_inner(n, carry, blocks):
+        for b in blocks:
+            enc1(2 * n + 1, 2 * n + 2, b)
+        return carry
+
+    lax.fori_loop(0, 3, functools.partial(enc1_inner, blocks=(1, 2)), 0)
+
+    got_w2.wait()
+    r, c = iota((64, 256), 0), iota((64, 256), 1)
+    spots = [ones_where(c == r + 64 * yo) for yo in range(4)]
+    taps = [cat([w2[pl.ds(9 * i + 3 * j, 3)].reshape(96, 64) for i in range(3)], 0) for j in range(3)]
+    for n, yi in enumerate((0, 1, 2, 3, -1, 4)):
+        t = None
+        for j in range(3):
+            if 0 <= yi + 1 - j < 4:
+                u = nn(taps[j], spots[yi + 1 - j])
+                t = u if t is None else t + u
+        t = t.astype(BF)
+        for i in range(3):
             for l in range(3):
-                for yo in range(4):
-                    j = yi - yo + 1
-                    row.append(w2[9 * i + 3 * j + l] if 0 <= j < 3 else z64)
-            k2[pl.ds(256 * i + 32 * n, 32), :] = cat(row, 1)
-    loads[3].wait()
+                k2[pl.ds(256 * i + 32 * n, 32), pl.ds(256 * l, 256)] = t[96 * i + 32 * l : 96 * i + 32 * l + 32]
+    for i in range(3):
+        k2[pl.ds(256 * i + 192, 64), :] = jnp.zeros((64, 768), BF)
+    got_w3.wait()
     z128 = jnp.zeros((64, 128), BF)
     for i in range(3):
         for n, yi in enumerate((0, 1, -1, 2)):
@@ -152,7 +189,27 @@
                         w3[9 * i + 3 * j + l] if 0 <= j < 3 else z128
                     )
 
-    arrive(x1)
+    arrive(x1[6:])
+
+    @pl.when(gy == 0)
+    def _():
+        fext[pl.ds(1, 8), pl.ds(0, 32)] = jnp.zeros((8, 32, 128), BF)
+
+    @pl.when(gy == ny - 1)
+    def _():
+        fext[pl.ds(1, 8), pl.ds(288, 32)] = jnp.zeros((8, 32, 128), BF)
+
+    lax.fori_loop(0, 3, functools.partial(enc1_inner, blocks=(0, 3)), 0)
+
+    def pool1(x):
+        a = e1[2 * x].astype(F32) + e1[2 * x + 1].astype(F32)
+        a = cat([a[64 * b : 64 * b + 32] + a[64 * b + 32 : 64 * b + 64] for b in range(4)], 0)
+        a = (a + pltpu.roll(a, 127, 1)) * 0.125
+        return a.astype(BF)
+
+    pick64 = ones_where(iota((64, 128), 1) == 2 * iota((64, 128), 0))
+    pooled = [None, pool1(1), pool1(2), None]
+    arrive(x1[:6])
 
     @pl.when(gx == 0)
     def _():
@@ -164,42 +221,22 @@
 
     @pl.when(gy == 0)
     def _():
-        fext[:, pl.ds(0, 32)] = jnp.zeros((10, 32, 128), BF)
+        for x in (0, 9):
+            fext[x, pl.ds(0, 32)] = jnp.zeros((32, 128), BF)
 
     @pl.when(gy == ny - 1)
     def _():
-        fext[:, pl.ds(288, 32)] = jnp.zeros((10, 32, 128), BF)
-
-    def enc1(x, carry):
-        for b in range(4):
-            rhs = cat(
-                [
-                    cat([fext[2 * x + i, pl.ds(64 * b, 128), :], fext[2 * x + 1 + i, pl.ds(64 * b, 128), :]], 1)
-                    for i in range(3)
-                ],
-                0,
-            )
-            t = nn(k1[...], rhs)
-            total = None
-            for h in range(2):
-                u = t[:, 128 * h : 128 * (h + 1)]
-                v = u[64:128] + shifted(u[:64], 1, 1, 128) + shifted(u[128:], -1, 1, 128)
-                v = gelu(v).astype(BF)
-                e1[2 * x + h, pl.ds(64 * b, 64), :] = v
-                f = v.astype(F32)
-                f = f[:32] + f[32:]
-                total = f if total is None else total + f
-            total = total + pltpu.roll(total, 127, 1)
-            pbs[x, pl.ds(32 * b, 32), :] = (total * 0.125).astype(BF)
-        return carry
-
-    lax.fori_loop(0, 4, enc1, 0)
-
-    pick64 = ones_where(iota((64, 128), 1) == 2 * iota((64, 128), 0))
+        for x in (0, 9):
+            fext[x, pl.ds(288, 32)] = jnp.zeros((32, 128), BF)
+
+    for b in range(4):
+        enc1(0, 7, b)
+    pooled[0], pooled[3] = pool1(0), pool1(3)
+
     for s, y in ((0, 0), (1, 96)):
-        y1s[s] = nt(pick64, cat([pbs[x, pl.ds(y, 32), :] for x in range(4)], 0)).astype(BF)
+        y1s[s] = nt(pick64, cat([p[y : y + 32] for p in pooled], 0)).astype(BF)
     for x in range(4):
-        p1[x + 1] = nt(pick64, pbs[x]).astype(BF)
+        p1[x + 1] = nt(pick64, pooled[x]).astype(BF)
 
     def halo(main, ys, yr, n_local, ss, rs):
         copies = []
@@ -214,6 +251,33 @@
 
     x2 = halo(p1, y1s, y1r, 4, s2, r2)
     start(x2)
+
+    got_v2.wait()
+    for px in range(2):
+        for py in range(2):
+            for tx in range(2):
+                for ty in range(2):
+                    s = []
+                    for l in range(3):
+                        terms = [
+                            v2[9 * i + 3 * j + l].astype(F32) for i in TAPS[px][tx] for j in TAPS[py][ty]
+                        ]
+                        s.append(functools.reduce(jnp.add, terms))
+                    block = cat([s[0], s[2], s[1] + s[2], s[0] + s[1]], 0).astype(BF)
+                    g2[pl.ds(256 * (2 * px + py), 256), pl.ds(128 * (2 * tx + ty), 128)] = block
+    got_v1.wait()
+    for px in range(2):
+        for py in range(2):
+            for l in range(3):
+                row = []
+                for tx in range(2):
+                    for ty in range(2):
+                        terms = [
+                            v1[9 * i + 3 * j + l].astype(F32) for i in TAPS[px][tx] for j in TAPS[py][ty]
+                        ]
+                        row.append(functools.reduce(jnp.add, terms).astype(BF))
+                g1[pl.ds(96 * (2 * px + py) + 32 * l, 32), :] = cat(row, 1)
+
     arrive(x2)
 
     def sides(yr, n_local, c):
@@ -312,33 +376,8 @@
     xe3 = cells(e3e, 2, se3, re3)
     start(xe3)
 
-    loads[6].wait()
-    for px in range(2):
-        for py in range(2):
-            for tx in range(2):
-                for ty in range(2):
-                    s = []
-                    for l in range(3):
-                        terms = [
-                            v2[9 * i + 3 * j + l].astype(F32) for i in TAPS[px][tx] for j in TAPS[py][ty]
-                        ]
-                        s.append(functools.reduce(jnp.add, terms))
-                    block = cat([s[0], s[2], s[1] + s[2], s[0] + s[1]], 0).astype(BF)
-                    g2[pl.ds(256 * (2 * px + py), 256), pl.ds(128 * (2 * tx + ty), 128)] = block
-    loads[7].wait()
-    for px in range(2):
-        for py in range(2):
-            for l in range(3):
-                row = []
-                for tx in range(2):
-                    for ty in range(2):
-                        terms = [
-                            v1[9 * i + 3 * j + l].astype(F32) for i in TAPS[px][tx] for j in TAPS[py][ty]
-                        ]
-                        row.append(functools.reduce(jnp.add, terms).astype(BF))
-                g1[pl.ds(96 * (2 * px + py) + 32 * l, 32), :] = cat(row, 1)
-
-    loads[4].wait()
+    for c in got_w4:
+        c.wait()
     for n, (dx, dy) in enumerate(window):
         pltpu.make_async_remote_copy(
             src_ref=p3.at[2, gy + 2], dst_ref=p3.at[2 - dx, lax.rem(gy - dy + ny, ny) + 2],
@@ -361,9 +400,7 @@
         ],
         0,
     )
-    t = cat(
-        [nt(lhs, cat([w4[9 * i + 3 * j + l] for i in range(3) for j in range(3)], 1)) for l in range(3)], 1
-    )
+    t = nt(lhs, k4[...])
     e4 = gelu(t[:, 256:512] + shifted(t[:, :256], 1, 0, 16) + shifted(t[:, 512:], -1, 0, 16))
 
     def inside(x, y, width, n_local):
@@ -383,7 +420,8 @@
 
     e4 = [kept(e4[16 * n : 16 * n + 16], inside(n // 3, n % 3, 16, 1)).astype(BF) for n in range(9)]
 
-    loads[5].wait()
+    for c in got_v3:
+        c.wait()
     twice = ones_where(iota((32, 16), 1) == iota((32, 16), 0) // 2)
     up = nn(twice, cat(e4, 1)).astype(BF)
     at = ((0, 0, 1), (0, 1, 1), (1, 1, 2), (1, 2, 2))
@@ -393,36 +431,35 @@
                 for j in range(3):
                     n = 3 * at[x][i] + at[y][j]
                     pd3[pl.ds(128 * x + 32 * y, 32), pl.ds(256 * (3 * i + j), 256)] = up[:, 256 * n : 256 * n + 256]
+    t = nt(pd3[...], kd3[...])
+    v = gelu(t[:, 128:256] + shifted(t[:, :128], 1, 0, 32) + shifted(t[:, 256:], -1, 0, 32))
     arrive(xe3)
     for x in range(4):
-        t = None
-        for i in range(3):
-            for j in range(3):
-                u = nt(
-                    pd3[pl.ds(128 * x, 128), pl.ds(256 * (3 * i + j), 256)],
-                    cat([v3[9 * i + 3 * j + l] for l in range(3)], 0),
-                )
-                t = u if t is None else t + u
-        v = gelu(t[:, 128:256] + shifted(t[:, :128], 1, 0, 32) + shifted(t[:, 256:], -1, 0, 32))
         for y in range(4):
-            w = v[32 * y : 32 * y + 32] + e3e[x, y].astype(F32)
+            n = 128 * x + 32 * y
+            w = v[n : n + 32] + e3e[x, y].astype(F32)
             d3e[x, y] = kept(w, inside(x, y, 32, 2)).astype(BF)
 
     arrive(xe2)
-    lane96 = iota((96, 128), 1) < 64
-    for k in range(3):
-        lhs = cat(
-            [cat([d3e[k, m], d3e[k, m + 1], d3e[k + 1, m], d3e[k + 1, m + 1]], 1) for m in range(3)], 0
-        )
-        t = nt(lhs, g2[...])
-        for px in range(2):
-            for py in range(2):
-                n = 256 * (2 * px + py)
-                a, b = t[:, n : n + 128], t[:, n + 128 : n + 256]
-                v = gelu(b + jnp.where(lane96, shifted(a, 1, 0, 32), shifted(a, -1, 0, 32)))
+    lane = iota((288, 128), 1) < 64
+    lhs = cat(
+        [
+            cat([d3e[k, m], d3e[k, m + 1], d3e[k + 1, m], d3e[k + 1, m + 1]], 1)
+            for k in range(3)
+            for m in range(3)
+        ],
+        0,
+    )
+    t = nt(lhs, g2[...])
+    for px in range(2):
+        for py in range(2):
+            n = 256 * (2 * px + py)
+            a, b = t[:, n : n + 128], t[:, n + 128 : n + 256]
+            v = gelu(b + jnp.where(lane, shifted(a, 1, 0, 32), shifted(a, -1, 0, 32)))
+            for k in range(3):
                 for m in range(3):
                     x, y = 2 * k + 1 - px, 2 * m + 1 - py
-                    w = v[32 * m : 32 * m + 32] + e2e[x, y].astype(F32)
+                    w = v[96 * k + 32 * m : 96 * k + 32 * m + 32] + e2e[x, y].astype(F32)
                     d2e[x, y] = kept(w, inside(x, y, 32, 4))
 
     rr, cc = iota((128, 64), 0), iota((128, 64), 1)
@@ -438,62 +475,61 @@
         for m in range(5):
             q[x, m] = a[:, 128 * m : 128 * m + 128]
 
+    done = []
     for k in range(5):
-        for m in range(5):
-            t = nt(g1[...], cat([q[k, m], q[k + 1, m]], 1))
+        for ms in ((0, 1), (2, 3), (4,)):
+            t = nt(g1[...], cat([cat([q[k, m], q[k + 1, m]], 1) for m in ms], 0))
             for px in range(2):
                 for py in range(2):
-                    a, b = k - px, m - py
-                    if not (0 <= a < 4 and 0 <= b < 4):
-                        continue
-                    x, y = 2 * a + px, 2 * b + py
-                    u = t[96 * (2 * px + py) : 96 * (2 * px + py) + 96]
-                    v = gelu(u[32:64] + shifted(u[:32], 1, 1, 128) + shifted(u[64:], -1, 1, 128))
-                    v = v + e1[x, pl.ds(32 * y, 32), :].astype(F32)
-                    dd[x, pl.ds(32 * y, 32), :] = v.astype(BF)
-
-    def back(x, carry):
-        t = nn(perm_t, cat([dd[2 * x], dd[2 * x + 1]], 1))
-        for h in range(2):
-            u = t[:, 128 * h : 128 * h + 128].reshape(32, 1, 8, 128).astype(BF)
-            ov[:, pl.ds(2 * x + h, 1)] = u
-        return carry
-
-    lax.fori_loop(0, 4, back, 0)
-    done = pltpu.make_async_copy(ov, out, osem)
-    done.start()
+                    for h, m in enumerate(ms):
+                        a, b = k - px, m - py
+                        if not (0 <= a < 4 and 0 <= b < 4):
+                            continue
+                        x, y = 2 * a + px, 2 * b + py
+                        n = 96 * (2 * px + py)
+                        u = t[n : n + 96, 128 * h : 128 * h + 128]
+                        v = gelu(u[32:64] + shifted(u[:32], 1, 1, 128) + shifted(u[64:], -1, 1, 128))
+                        v = v + e1[x, pl.ds(32 * y, 32), :].astype(F32)
+                        dd[x, y] = v.astype(BF)
+        for x in (2 * k - 1, 2 * k):
+            if 0 <= x < 8:
+                c = pltpu.make_async_copy(dd.at[x], out.at[x], osem.at[x])
+                c.start()
+                done.append(c)
+
     for copies in (x1, x2, x3, x4, xe2, xe3):
         for c in copies:
             c.wait_send()
-    done.wait()
+    for c in done:
+        c.wait()
 
 
 def local(features, w_enc1, w_enc2, w_enc3, w_enc4, w_dec3, w_dec2, w_dec1):
     w_enc2, w_enc3 = jnp.swapaxes(w_enc2, 1, 2), jnp.swapaxes(w_enc3, 1, 2)
+    w_enc4, w_dec3 = w_enc4.reshape(9, 768, 128), w_dec3.reshape(9, 384, 256)
     args = (features, w_enc1, w_enc2, w_enc3, w_enc4, w_dec3, w_dec2, w_dec1)
     ny = lax.axis_size("gy")
     far = 5 * ny - 1
     dma = pltpu.SemaphoreType.DMA
-    scratch = [pltpu.VMEM(a.shape, BF) for a in args]
-    scratch.append(pltpu.VMEM((32, 8, 8, 128), BF))
+    scratch = [pltpu.VMEM(a.shape, BF) for a in (features, w_enc1, w_enc2, w_enc3, w_dec2, w_dec1)]
     for shape in (
-        (10, 320, 128), (8, 256, 128), (4, 128, 128),
+        (10, 320, 128), (8, 256, 128),
         (6, 64, 128), (2, 64, 128), (2, 3, 64, 128),
         (4, 32, 128), (2, 32, 128), (2, 3, 32, 128),
         (5, ny + 4, 16, 128), (6, 6, 32, 128), (4, 4, 32, 128),
-        (192, 384), (768, 768), (768, 768), (1024, 512), (384, 256),
+        (192, 384), (768, 768), (768, 768), (768, 1152), (384, 2304), (1024, 512), (384, 256),
         (512, 2304), (4, 4, 32, 128),
     ):
         scratch.append(pltpu.VMEM(shape, BF))
     scratch.append(pltpu.VMEM((6, 6, 32, 128), F32))
     scratch.append(pltpu.VMEM((6, 5, 128, 128), BF))
-    scratch.append(pltpu.VMEM((8, 256, 128), BF))
-    scratch += [dma((8,)), dma]
+    scratch.append(pltpu.VMEM((8, 8, 32, 128), BF))
+    scratch += [dma((24,)), dma((8,))]
     for n in (8, 8, 8, far, 8, 8):
         scratch += [dma((n,)), dma((n,))]
-    return pl.pallas_call(
+    decoded = pl.pallas_call(
         kernel,
-        out_shape=jax.ShapeDtypeStruct(features.shape, BF),
+        out_shape=jax.ShapeDtypeStruct((8, 8, 32, 128), BF),
         in_specs=[pl.BlockSpec(memory_space=pl.ANY)] * 8,
         out_specs=pl.BlockSpec(memory_space=pl.ANY),
         scratch_shapes=scratch,
@@ -502,6 +538,7 @@
         ),
         cost_estimate=pl.CostEstimate(flops=2 * 1115000000, bytes_accessed=7000000, transcendentals=1000000),
     )(*args)
+    return jnp.transpose(decoded, (2, 0, 1, 3))
 
 
 def solution(mesh):

time: 45.7 us -> 40.2 us (0.88)
  Pallas kernels: 43.7 us -> 38 us
    pallas_call x1, Pallas kernels: 43.7 us -> 38 us  [local(): pl.pallas_call(kernel, out_shape=jax.ShapeDtypeStruct((8, 8, 32, 128), BF...]
    transpose x0 -> x1, local copies, waits for them, and re-layouts: none -> 2.04 us  [local(): return jnp.transpose(decoded, (2, 0, 1, 3))]
    unnamed x1 -> x0, local copies, waits for them, and re-layouts: 1.87 us -> none
where the time goes in v2:
time: 40.2 us; the launch traced here: 40 us
  Pallas kernels  38 us (95%)
  local copies, waits for them, and re-layouts  2.04 us (5%)
    pallas_call x1, Pallas kernels, local(): pl.pallas_call(kernel, out_shape=jax.ShapeDtypeStruct((8, 8, 32, 128), BF...  38 us
    transpose x1, local copies, waits for them, and re-layouts, local(): return jnp.transpose(decoded, (2, 0, 1, 3))  2.04 us

profile of v2, /device:TPU:1, one launch (start us, length us, event | category | flops | bytes accessed | tf_op | source)
XLA Modules:
  0.0 40.0 jit_solution(14281210906920729527)
XLA Ops:
  0.0 38.0 %shard_map.82 = bf16[8,8,32,128]{3,2,1,0:T(8,128)(2,1)} custom-call(bf16[32,8,8,128]{3,2,1,0:T(8,128)(2,1)} %feat.1, bf16[27,32,32]{2,1,0:T(8,128)(2,1)} %w1h.1, bf16[27,32,64]{2,1,0:T(8,128)(2,1)} %bitcast.9, bf16[27,64,128]{2,1,0:T(8,128)(2,1)} %bitcast.8, bf16[9,768,128]{2,1,0:T(8,128)(2,1)} %bitcast.6, bf16[9,384,256]{2,1,0:T(8,128)(2,1)} %bitcast.7, ...), custom_call_target="tpu_custom_call" | custom-call | flops 2230000128 | bytes 7000000 | tf_op jit(solution)/shard_map/pallas_call | solution.py:530
  38.0 2.0 %copy.9 = bf16[32,8,8,128]{3,2,1,0:T(8,128)(2,1)} copy(bf16[32,8,8,128]{3,0,2,1:T(8,128)(2,1)} %bitcast.5) | data formatting | bytes 1048576 | tf_op jit(solution)/shard_map/transpose | solution.py:541

commit v3 on v2

--- a/solution.py
+++ b/solution.py
@@ -56,9 +56,9 @@
 def kernel(
     feat, w1h, w2h, w3h, w4h, v3h, v2h, v1h, out,
     fv, w1, w2, w3, v2, v1,
-    fext, e1, p1, y1s, y1r, p2, y2s, y2r, p3, e2e, e3e,
+    fext, e1, p1, p3, e2e, e3e,
     k1, k2, k3, k4, kd3, g2, g1, pd3, d3e, d2e, q, dd,
-    lsem, osem, s1, r1, s2, r2, s3, r3, s4, r4, se2, re2, se3, re3,
+    lsem, osem, s1, r1, s2, r2, s4, r4, se3, re3,
 ):
     gx, gy = lax.axis_index("gx"), lax.axis_index("gy")
     nx, ny = lax.axis_size("gx"), lax.axis_size("gy")
@@ -166,26 +166,27 @@
     r, c = iota((64, 256), 0), iota((64, 256), 1)
     spots = [ones_where(c == r + 64 * yo) for yo in range(4)]
     taps = [cat([w2[pl.ds(9 * i + 3 * j, 3)].reshape(96, 64) for i in range(3)], 0) for j in range(3)]
-    for n, yi in enumerate((0, 1, 2, 3, -1, 4)):
+    for yi in range(1, 7):
         t = None
         for j in range(3):
-            if 0 <= yi + 1 - j < 4:
-                u = nn(taps[j], spots[yi + 1 - j])
+            if 0 <= yi - 1 - j < 4:
+                u = nn(taps[j], spots[yi - 1 - j])
                 t = u if t is None else t + u
         t = t.astype(BF)
         for i in range(3):
             for l in range(3):
-                k2[pl.ds(256 * i + 32 * n, 32), pl.ds(256 * l, 256)] = t[96 * i + 32 * l : 96 * i + 32 * l + 32]
+                k2[pl.ds(256 * i + 32 * yi, 32), pl.ds(256 * l, 256)] = t[96 * i + 32 * l : 96 * i + 32 * l + 32]
     for i in range(3):
-        k2[pl.ds(256 * i + 192, 64), :] = jnp.zeros((64, 768), BF)
+        for yi in (0, 7):
+            k2[pl.ds(256 * i + 32 * yi, 32), :] = jnp.zeros((32, 768), BF)
     got_w3.wait()
     z128 = jnp.zeros((64, 128), BF)
     for i in range(3):
-        for n, yi in enumerate((0, 1, -1, 2)):
+        for yi in range(4):
             for l in range(3):
                 for yo in range(2):
-                    j = yi - yo + 1
-                    k3[pl.ds(256 * i + 64 * n, 64), pl.ds(256 * l + 128 * yo, 128)] = (
+                    j = yi - yo
+                    k3[pl.ds(256 * i + 64 * yi, 64), pl.ds(256 * l + 128 * yo, 128)] = (
                         w3[9 * i + 3 * j + l] if 0 <= j < 3 else z128
                     )
 
@@ -233,23 +234,13 @@
         enc1(0, 7, b)
     pooled[0], pooled[3] = pool1(0), pool1(3)
 
-    for s, y in ((0, 0), (1, 96)):
-        y1s[s] = nt(pick64, cat([p[y : y + 32] for p in pooled], 0)).astype(BF)
+    t = nt(pick64, cat(pooled, 0)).astype(BF)
     for x in range(4):
-        p1[x + 1] = nt(pick64, pooled[x]).astype(BF)
-
-    def halo(main, ys, yr, n_local, ss, rs):
-        copies = []
-        for n, (dx, dy) in enumerate(DIRS):
-            if dy == 0:
-                sx, tx, _ = side(dx, n_local)
-                copies.append(send(n, dx, dy, main.at[sx], main.at[tx], ss, rs))
-            else:
-                s = 1 if dy == 1 else 0
-                copies.append(send(n, dx, dy, ys.at[s], yr.at[1 - s, 1 - dx], ss, rs))
-        return copies
-
-    x2 = halo(p1, y1s, y1r, 4, s2, r2)
+        p1[1, x + 3] = t[:, 128 * x : 128 * x + 128]
+    x2 = []
+    for n, (dx, dy) in enumerate(DIRS):
+        sx, tx, cx = ((3, 7, 3), (3, 3, 4), (4, 0, 3))[dx + 1]
+        x2.append(send(n, dx, dy, p1.at[1, pl.ds(sx, cx)], p1.at[1 - dy, pl.ds(tx, cx)], s2, r2))
     start(x2)
 
     got_v2.wait()
@@ -280,84 +271,54 @@
 
     arrive(x2)
 
-    def sides(yr, n_local, c):
-        found = []
-        for x in range(n_local + 2):
-            slot, at = (0, n_local - 1) if x == 0 else (2, 0) if x == n_local + 1 else (1, x - 1)
-            inside = (gx > 0) if x == 0 else (gx < nx - 1) if x == n_local + 1 else True
-            lo = yr[0, slot][:, at * c : (at + 1) * c]
-            hi = yr[1, slot][:, at * c : (at + 1) * c]
-            zero = jnp.zeros_like(lo)
-            lo = jnp.where(inside & (gy > 0), lo, zero)
-            hi = jnp.where(inside & (gy < ny - 1), hi, zero)
-            parts = [lo, hi]
-            if c < 64:
-                parts.append(jnp.zeros((lo.shape[0], 128 - 2 * c), BF))
-            found.append(cat(parts, 1))
-        return found
-
-    def mains(main, n_local):
-        found = []
-        for x in range(n_local + 2):
-            v = main[x]
-            if x == 0:
-                v = jnp.where(gx > 0, v, jnp.zeros_like(v))
-            if x == n_local + 1:
-                v = jnp.where(gx < nx - 1, v, jnp.zeros_like(v))
-            found.append(v)
-        return found
-
-    m1, h1 = mains(p1, 4), sides(y1r, 4, 32)
-    lhs = cat([cat([cat([m1[x + i], h1[x + i]], 1) for i in range(3)], 1) for x in range(4)], 0)
-    t = nn(lhs, k2[...])
-    e2 = gelu(t[:, 256:512] + shifted(t[:, :256], 1, 0, 64) + shifted(t[:, 512:], -1, 0, 64)).astype(BF)
-    f = e2.astype(F32)
+    @pl.when(gx == 0)
+    def _():
+        p1[:, pl.ds(0, 3)] = jnp.zeros((3, 3, 64, 128), BF)
+
+    @pl.when(gx == nx - 1)
+    def _():
+        p1[:, pl.ds(7, 3)] = jnp.zeros((3, 3, 64, 128), BF)
+
+    @pl.when(gy == 0)
+    def _():
+        p1[0] = jnp.zeros((10, 64, 128), BF)
+
+    @pl.when(gy == ny - 1)
+    def _():
+        p1[2] = jnp.zeros((10, 64, 128), BF)
+
     low = iota((64, 128), 1) < 64
+    e2 = []
+    pairs = []
+    for g in range(2):
+        lhs = cat(
+            [cat([cat([p1[g, x + i], p1[g + 1, x + i]], 1) for i in range(3)], 1) for x in range(8)], 0
+        )
+        t = nn(lhs, k2[...])
+        t = gelu(t[:, 256:512] + shifted(t[:, :256], 1, 0, 64) + shifted(t[:, 512:], -1, 0, 64))
+        rows = []
+        for x in range(8):
+            v = t[64 * x : 64 * x + 64]
+            halves = [v[:, :128], v[:, 128:]]
+            for h in range(2):
+                ok = True if h != g else (gy > 0) if g == 0 else (gy < ny - 1)
+                if x < 2:
+                    ok = ok & (gx > 0)
+                if x > 5:
+                    ok = ok & (gx < nx - 1)
+                if ok is not True:
+                    halves[h] = jnp.where(ok, halves[h], jnp.zeros_like(halves[h]))
+            rows.append([v.astype(BF) for v in halves])
+        e2.append(rows)
+        for x in range(4):
+            a0, a1 = [rows[2 * x][h].astype(F32) + rows[2 * x + 1][h].astype(F32) for h in range(2)]
+            a = jnp.where(low, a0 + pltpu.roll(a0, 64, 1), a1 + pltpu.roll(a1, 64, 1))
+            pairs.append(((a + pltpu.roll(a, 63, 0)) * 0.125).astype(BF))
     pick32 = ones_where(iota((32, 64), 1) == 2 * iota((32, 64), 0))
-    p2v = []
-    for x in range(2):
-        a = f[128 * x : 128 * x + 64] + f[128 * x + 64 : 128 * x + 128]
-        a0, a1 = a[:, :128], a[:, 128:]
-        a = jnp.where(low, a0 + pltpu.roll(a0, 64, 1), a1 + pltpu.roll(a1, 64, 1))
-        a = (a + pltpu.roll(a, 63, 0)) * 0.125
-        a = nn(pick32, a.astype(BF))
-        p2v.append(a)
-        p2[x + 1] = a.astype(BF)
-    low32 = iota((32, 128), 1) < 64
-    y2s[0] = jnp.where(low32, p2v[0], pltpu.roll(p2v[1], 64, 1)).astype(BF)
-    y2s[1] = jnp.where(low32, pltpu.roll(p2v[0], 64, 1), p2v[1]).astype(BF)
-    x3 = halo(p2, y2s, y2r, 2, s3, r3)
-    start(x3)
-
-    rr, cc = iota((64, 64), 0), iota((64, 64), 1)
-    split = ones_where(cc == 2 * (rr % 32) + rr // 32)
-    for x in range(4):
-        a = nn(split, e2[64 * x : 64 * x + 64])
-        for y in range(4):
-            ev = a[:32, 128 * (y // 2) : 128 * (y // 2) + 128]
-            od = a[32:, 128 * (y // 2) : 128 * (y // 2) + 128]
-            if y % 2 == 0:
-                cell = jnp.where(low32, ev, pltpu.roll(od, 64, 1))
-            else:
-                cell = jnp.where(low32, pltpu.roll(ev, 64, 1), od)
-            e2e[x + 1, y + 1] = cell.astype(BF)
-
-    def cells(ref, n_local, ss, rs):
-        copies = []
-        for n, (dx, dy) in enumerate(DIRS):
-            sx, tx, cx = side(dx, n_local)
-            sy, ty, cy = side(dy, n_local)
-            copies.append(
-                send(n, dx, dy, ref.at[pl.ds(sx, cx), pl.ds(sy, cy)], ref.at[pl.ds(tx, cx), pl.ds(ty, cy)], ss, rs)
-            )
-        return copies
-
-    xe2 = cells(e2e, 4, se2, re2)
-    start(xe2)
-    arrive(x3)
-
-    m2, h2 = mains(p2, 2), sides(y2r, 2, 64)
-    lhs = cat([cat([cat([m2[x + i], h2[x + i]], 1) for i in range(3)], 1) for x in range(2)], 0)
+    t = nn(pick32, cat(pairs, 1)).astype(BF)
+    p2 = [cat([t[:, 128 * x : 128 * x + 128], t[:, 512 + 128 * x : 512 + 128 * x + 128]], 1) for x in range(4)]
+
+    lhs = cat([cat([p2[x + i] for i in range(3)], 1) for x in range(2)], 0)
     t = nn(lhs, k3[...])
     e3 = gelu(t[:, 256:512] + shifted(t[:, :256], 1, 0, 32) + shifted(t[:, 512:], -1, 0, 32)).astype(BF)
     f = e3.astype(F32)
@@ -373,8 +334,32 @@
     for x in range(2):
         for y in range(2):
             e3e[x + 1, y + 1] = e3[32 * x : 32 * x + 32, 128 * y : 128 * y + 128]
+    def cells(ref, n_local, ss, rs):
+        copies = []
+        for n, (dx, dy) in enumerate(DIRS):
+            sx, tx, cx = side(dx, n_local)
+            sy, ty, cy = side(dy, n_local)
+            copies.append(
+                send(n, dx, dy, ref.at[pl.ds(sx, cx), pl.ds(sy, cy)], ref.at[pl.ds(tx, cx), pl.ds(ty, cy)], ss, rs)
+            )
+        return copies
+
     xe3 = cells(e3e, 2, se3, re3)
     start(xe3)
+
+    low32 = iota((32, 128), 1) < 64
+    rr, cc = iota((64, 64), 0), iota((64, 64), 1)
+    split = ones_where(cc == 2 * (rr % 32) + rr // 32)
+    for x in range(6):
+        t = nn(split, cat([e2[g][x + 1][h] for g in range(2) for h in range(2)], 1))
+        for y in range(6):
+            n = 128 * ((y + 1) // 2)
+            ev, od = t[:32, n : n + 128], t[32:, n : n + 128]
+            if y % 2 == 1:
+                cell = jnp.where(low32, ev, pltpu.roll(od, 64, 1))
+            else:
+                cell = jnp.where(low32, pltpu.roll(ev, 64, 1), od)
+            e2e[x, y] = cell.astype(BF)
 
     for c in got_w4:
         c.wait()
@@ -400,8 +385,11 @@
         ],
         0,
     )
-    t = nt(lhs, k4[...])
-    e4 = gelu(t[:, 256:512] + shifted(t[:, :256], 1, 0, 16) + shifted(t[:, 512:], -1, 0, 16))
+    t = nt(k4[...], lhs)
+    e4 = gelu(t[256:512] + shifted(t[:256], 1, 1, 16) + shifted(t[512:], -1, 1, 16))
+    n = iota((256, 144), 1) // 16
+    x, y = gx - 1 + n // 3, gy - 1 + n % 3
+    e4 = jnp.where((x >= 0) & (x < nx) & (y >= 0) & (y < ny), e4, 0.0).astype(BF)
 
     def inside(x, y, width, n_local):
         ok = True
@@ -418,19 +406,17 @@
     def kept(v, ok):
         return v if ok is True else jnp.where(ok, v, jnp.zeros_like(v))
 
-    e4 = [kept(e4[16 * n : 16 * n + 16], inside(n // 3, n % 3, 16, 1)).astype(BF) for n in range(9)]
 
     for c in got_v3:
         c.wait()
-    twice = ones_where(iota((32, 16), 1) == iota((32, 16), 0) // 2)
-    up = nn(twice, cat(e4, 1)).astype(BF)
+    up = nt(ones_where(iota((288, 144), 1) == iota((288, 144), 0) // 2), e4).astype(BF)
     at = ((0, 0, 1), (0, 1, 1), (1, 1, 2), (1, 2, 2))
     for x in range(4):
         for y in range(4):
             for i in range(3):
                 for j in range(3):
                     n = 3 * at[x][i] + at[y][j]
-                    pd3[pl.ds(128 * x + 32 * y, 32), pl.ds(256 * (3 * i + j), 256)] = up[:, 256 * n : 256 * n + 256]
+                    pd3[pl.ds(128 * x + 32 * y, 32), pl.ds(256 * (3 * i + j), 256)] = up[32 * n : 32 * n + 32]
     t = nt(pd3[...], kd3[...])
     v = gelu(t[:, 128:256] + shifted(t[:, :128], 1, 0, 32) + shifted(t[:, 256:], -1, 0, 32))
     arrive(xe3)
@@ -440,7 +426,6 @@
             w = v[n : n + 32] + e3e[x, y].astype(F32)
             d3e[x, y] = kept(w, inside(x, y, 32, 2)).astype(BF)
 
-    arrive(xe2)
     lane = iota((288, 128), 1) < 64
     lhs = cat(
         [
@@ -497,7 +482,7 @@
                 c.start()
                 done.append(c)
 
-    for copies in (x1, x2, x3, x4, xe2, xe3):
+    for copies in (x1, x2, x4, xe3):
         for c in copies:
             c.wait_send()
     for c in done:
@@ -514,8 +499,7 @@
     scratch = [pltpu.VMEM(a.shape, BF) for a in (features, w_enc1, w_enc2, w_enc3, w_dec2, w_dec1)]
     for shape in (
         (10, 320, 128), (8, 256, 128),
-        (6, 64, 128), (2, 64, 128), (2, 3, 64, 128),
-        (4, 32, 128), (2, 32, 128), (2, 3, 32, 128),
+        (3, 10, 64, 128),
         (5, ny + 4, 16, 128), (6, 6, 32, 128), (4, 4, 32, 128),
         (192, 384), (768, 768), (768, 768), (768, 1152), (384, 2304), (1024, 512), (384, 256),
         (512, 2304), (4, 4, 32, 128),
@@ -525,7 +509,7 @@
     scratch.append(pltpu.VMEM((6, 5, 128, 128), BF))
     scratch.append(pltpu.VMEM((8, 8, 32, 128), BF))
     scratch += [dma((24,)), dma((8,))]
-    for n in (8, 8, 8, far, 8, 8):
+    for n in (8, 8, far, 8):
         scratch += [dma((n,)), dma((n,))]
     decoded = pl.pallas_call(
         kernel,

time: 40.2 us -> 36.7 us (0.913)
  Pallas kernels: 38 us -> 34.5 us
    pallas_call x1, Pallas kernels: 38 us -> 34.5 us  [local(): pl.pallas_call(kernel, out_shape=jax.ShapeDtypeStruct((8, 8, 32, 128), BF...]
where the time goes in v3:
time: 36.7 us; the launch traced here: 36.6 us
  Pallas kernels  34.5 us (94%)
  local copies, waits for them, and re-layouts  2.04 us (6%)
    pallas_call x1, Pallas kernels, local(): pl.pallas_call(kernel, out_shape=jax.ShapeDtypeStruct((8, 8, 32, 128), BF...  34.5 us
    transpose x1, local copies, waits for them, and re-layouts, local(): return jnp.transpose(decoded, (2, 0, 1, 3))  2.04 us

profile of v3, /device:TPU:1, one launch (start us, length us, event | category | flops | bytes accessed | tf_op | source)
XLA Modules:
  0.0 36.6 jit_solution(3972866395062698374)
XLA Ops:
  0.0 34.5 %shard_map.82 = bf16[8,8,32,128]{3,2,1,0:T(8,128)(2,1)} custom-call(bf16[32,8,8,128]{3,2,1,0:T(8,128)(2,1)} %feat.1, bf16[27,32,32]{2,1,0:T(8,128)(2,1)} %w1h.1, bf16[27,32,64]{2,1,0:T(8,128)(2,1)} %bitcast.9, bf16[27,64,128]{2,1,0:T(8,128)(2,1)} %bitcast.8, bf16[9,768,128]{2,1,0:T(8,128)(2,1)} %bitcast.6, bf16[9,384,256]{2,1,0:T(8,128)(2,1)} %bitcast.7, ...), custom_call_target="tpu_custom_call" | custom-call | flops 2230000128 | bytes 7000000 | tf_op jit(solution)/shard_map/pallas_call | solution.py:514
  34.6 2.0 %copy.9 = bf16[32,8,8,128]{3,2,1,0:T(8,128)(2,1)} copy(bf16[32,8,8,128]{3,0,2,1:T(8,128)(2,1)} %bitcast.5) | data formatting | bytes 1048576 | tf_op jit(solution)/shard_map/transpose | solution.py:525

commit v4 on v3

--- a/solution.py
+++ b/solution.py
@@ -57,8 +57,8 @@
     feat, w1h, w2h, w3h, w4h, v3h, v2h, v1h, out,
     fv, w1, w2, w3, v2, v1,
     fext, e1, p1, p3, e2e, e3e,
-    k1, k2, k3, k4, kd3, g2, g1, pd3, d3e, d2e, q, dd,
-    lsem, osem, s1, r1, s2, r2, s4, r4, se3, re3,
+    k1, k2, k3, k4, kd3, g2, g1, pd3, d3e, d2e, q,
+    lsem, s1, r1, s2, r2, s4, r4, se3, re3,
 ):
     gx, gy = lax.axis_index("gx"), lax.axis_index("gy")
     nx, ny = lax.axis_size("gx"), lax.axis_size("gy")
@@ -460,7 +460,6 @@
         for m in range(5):
             q[x, m] = a[:, 128 * m : 128 * m + 128]
 
-    done = []
     for k in range(5):
         for ms in ((0, 1), (2, 3), (4,)):
             t = nt(g1[...], cat([cat([q[k, m], q[k + 1, m]], 1) for m in ms], 0))
@@ -475,18 +474,10 @@
                         u = t[n : n + 96, 128 * h : 128 * h + 128]
                         v = gelu(u[32:64] + shifted(u[:32], 1, 1, 128) + shifted(u[64:], -1, 1, 128))
                         v = v + e1[x, pl.ds(32 * y, 32), :].astype(F32)
-                        dd[x, y] = v.astype(BF)
-        for x in (2 * k - 1, 2 * k):
-            if 0 <= x < 8:
-                c = pltpu.make_async_copy(dd.at[x], out.at[x], osem.at[x])
-                c.start()
-                done.append(c)
-
+                        out[x, y] = v.astype(BF)
     for copies in (x1, x2, x4, xe3):
         for c in copies:
             c.wait_send()
-    for c in done:
-        c.wait()
 
 
 def local(features, w_enc1, w_enc2, w_enc3, w_enc4, w_dec3, w_dec2, w_dec1):
@@ -507,21 +498,20 @@
         scratch.append(pltpu.VMEM(shape, BF))
     scratch.append(pltpu.VMEM((6, 6, 32, 128), F32))
     scratch.append(pltpu.VMEM((6, 5, 128, 128), BF))
-    scratch.append(pltpu.VMEM((8, 8, 32, 128), BF))
-    scratch += [dma((24,)), dma((8,))]
+    scratch.append(dma((24,)))
     for n in (8, 8, far, 8):
         scratch += [dma((n,)), dma((n,))]
     decoded = pl.pallas_call(
         kernel,
-        out_shape=jax.ShapeDtypeStruct((8, 8, 32, 128), BF),
+        out_shape=pltpu.VMEM((8, 8, 32, 128), BF),
         in_specs=[pl.BlockSpec(memory_space=pl.ANY)] * 8,
-        out_specs=pl.BlockSpec(memory_space=pl.ANY),
+        out_specs=pl.BlockSpec(memory_space=pltpu.VMEM),
         scratch_shapes=scratch,
         compiler_params=pltpu.CompilerParams(
-            collective_id=0, has_side_effects=True, vmem_limit_bytes=56 * 1024 * 1024
+            collective_id=0, has_side_effects=True, vmem_limit_bytes=48 * 1024 * 1024
         ),
         cost_estimate=pl.CostEstimate(flops=2 * 1115000000, bytes_accessed=7000000, transcendentals=1000000),
-    )(*args)
+    )(*[pltpu.with_memory_space_constraint(a, pltpu.HBM) for a in args])
     return jnp.transpose(decoded, (2, 0, 1, 3))
 
 

time: 36.7 us -> 35 us (0.954)
  local copies, waits for them, and re-layouts: 2.04 us -> 1 us
  Pallas kernels: 34.5 us -> 33.9 us
    transpose x1, local copies, waits for them, and re-layouts: 2.04 us -> 1 us  [local(): return jnp.transpose(decoded, (2, 0, 1, 3))]
    pallas_call x1, Pallas kernels: 34.5 us -> 33.9 us  [local(): pl.pallas_call(kernel, out_shape=pltpu.VMEM((8, 8, 32, 128), BF), in_spec...]
where the time goes in v4:
time: 35 us; the launch traced here: 34.9 us
  Pallas kernels  33.9 us (97%)
  local copies, waits for them, and re-layouts  1 us (3%)
    pallas_call x1, Pallas kernels, local(): pl.pallas_call(kernel, out_shape=pltpu.VMEM((8, 8, 32, 128), BF), in_spec...  33.9 us
    transpose x1, local copies, waits for them, and re-layouts, local(): return jnp.transpose(decoded, (2, 0, 1, 3))  1 us

profile of v4, /device:TPU:1, one launch (start us, length us, event | category | flops | bytes accessed | tf_op | source)
XLA Modules:
  0.0 34.9 jit_solution(1407147441586946670)
XLA Ops:
  0.0 33.9 %shard_map.82 = bf16[8,8,32,128]{3,2,1,0:T(8,128)(2,1)S(1)} custom-call(bf16[32,8,8,128]{3,2,1,0:T(8,128)(2,1)} %feat.1, bf16[27,32,32]{2,1,0:T(8,128)(2,1)} %w1h.1, bf16[27,32,64]{2,1,0:T(8,128)(2,1)} %bitcast.9, bf16[27,64,128]{2,1,0:T(8,128)(2,1)} %bitcast.8, bf16[9,768,128]{2,1,0:T(8,128)(2,1)} %bitcast.6, bf16[9,384,256]{2,1,0:T(8,128)(2,1)} %bitcast.7, ...), custom_call_target="tpu_custom_call" | custom-call | flops 2230000128 | bytes 7000000 | tf_op jit(solution)/shard_map/pallas_call | solution.py:504
  33.9 1.0 %copy.9 = bf16[32,8,8,128]{3,2,1,0:T(8,128)(2,1)} copy(bf16[32,8,8,128]{3,0,2,1:T(8,128)(2,1)S(1)} %bitcast.5) | data formatting | bytes 1048576 | tf_op jit(solution)/shard_map/transpose | solution.py:515

commit v5 on v4

--- a/solution.py
+++ b/solution.py
@@ -31,7 +31,8 @@
 
 
 def gelu(x):
-    return 0.5 * x * (1.0 + jnp.tanh(0.7978845608028654 * (x + 0.044715 * (x * x * x))))
+    half = 0.5 * x
+    return half + half * jnp.tanh(x * (0.7978845608028654 + 0.035677408136300125 * (x * x)))
 
 
 def shifted(v, step, axis, period):
@@ -57,8 +58,8 @@
     feat, w1h, w2h, w3h, w4h, v3h, v2h, v1h, out,
     fv, w1, w2, w3, v2, v1,
     fext, e1, p1, p3, e2e, e3e,
-    k1, k2, k3, k4, kd3, g2, g1, pd3, d3e, d2e, q,
-    lsem, s1, r1, s2, r2, s4, r4, se3, re3,
+    k1, k2, k3, k4, kd3, g2, g1, pd3, g3, d3e, d2e, q,
+    lsem, s1, r1, s2, r2, sp, rp, s4, r4, se3, re3,
 ):
     gx, gy = lax.axis_index("gx"), lax.axis_index("gy")
     nx, ny = lax.axis_size("gx"), lax.axis_size("gy")
@@ -210,37 +211,52 @@
 
     pick64 = ones_where(iota((64, 128), 1) == 2 * iota((64, 128), 0))
     pooled = [None, pool1(1), pool1(2), None]
-    arrive(x1[:6])
+    arrive(x1[4:6])
 
     @pl.when(gx == 0)
     def _():
-        fext[0] = jnp.zeros((320, 128), BF)
+        fext[0, pl.ds(32, 256)] = jnp.zeros((256, 128), BF)
 
     @pl.when(gx == nx - 1)
     def _():
-        fext[9] = jnp.zeros((320, 128), BF)
-
-    @pl.when(gy == 0)
-    def _():
-        for x in (0, 9):
-            fext[x, pl.ds(0, 32)] = jnp.zeros((32, 128), BF)
-
-    @pl.when(gy == ny - 1)
-    def _():
-        for x in (0, 9):
-            fext[x, pl.ds(288, 32)] = jnp.zeros((32, 128), BF)
-
-    for b in range(4):
-        enc1(0, 7, b)
+        fext[9, pl.ds(32, 256)] = jnp.zeros((256, 128), BF)
+
+    enc1(0, 7, 1)
+    enc1(0, 7, 2)
+    arrive(x1[:4])
+
+    @pl.when((gx == 0) | (gy == 0))
+    def _():
+        fext[0, pl.ds(0, 32)] = jnp.zeros((32, 128), BF)
+
+    @pl.when((gx == 0) | (gy == ny - 1))
+    def _():
+        fext[0, pl.ds(288, 32)] = jnp.zeros((32, 128), BF)
+
+    @pl.when((gx == nx - 1) | (gy == 0))
+    def _():
+        fext[9, pl.ds(0, 32)] = jnp.zeros((32, 128), BF)
+
+    @pl.when((gx == nx - 1) | (gy == ny - 1))
+    def _():
+        fext[9, pl.ds(288, 32)] = jnp.zeros((32, 128), BF)
+
+    enc1(0, 7, 0)
+    enc1(0, 7, 3)
     pooled[0], pooled[3] = pool1(0), pool1(3)
 
     t = nt(pick64, cat(pooled, 0)).astype(BF)
     for x in range(4):
         p1[1, x + 3] = t[:, 128 * x : 128 * x + 128]
+    odd = lax.rem(gx, 2)
+    mate = 1 - 2 * odd
     x2 = []
-    for n, (dx, dy) in enumerate(DIRS):
-        sx, tx, cx = ((3, 7, 3), (3, 3, 4), (4, 0, 3))[dx + 1]
-        x2.append(send(n, dx, dy, p1.at[1, pl.ds(sx, cx)], p1.at[1 - dy, pl.ds(tx, cx)], s2, r2))
+    for n, dy in enumerate((-1, 1)):
+        x2.append(send(n, -mate, dy, p1.at[1, pl.ds(3 + odd, 3)], p1.at[1 - dy, pl.ds(7 - 7 * odd, 3)], s2, r2))
+    for n, dy in enumerate((-1, 1)):
+        x2.append(send(2 + n, 0, dy, p1.at[1, pl.ds(3, 4)], p1.at[1 - dy, pl.ds(3, 4)], s2, r2))
+    x2.append(send(4, -1, 0, p1.at[1, pl.ds(3, 3)], p1.at[1, pl.ds(7, 3)], s2, r2))
+    x2.append(send(5, 1, 0, p1.at[1, pl.ds(4, 3)], p1.at[1, pl.ds(0, 3)], s2, r2))
     start(x2)
 
     got_v2.wait()
@@ -269,7 +285,66 @@
                         row.append(functools.reduce(jnp.add, terms).astype(BF))
                 g1[pl.ds(96 * (2 * px + py) + 32 * l, 32), :] = cat(row, 1)
 
-    arrive(x2)
+    for c in got_v3:
+        c.wait()
+
+    def sum_taps(n, carry):
+        rows = pl.ds(pl.multiple_of(32 * n, 32), 32)
+        lower = pl.ds(pl.multiple_of(384 + 32 * n, 32), 32)
+        taps = [kd3[rows, 768 * i : 768 * i + 768] for i in range(3)]
+        g3[rows, :768] = taps[0]
+        g3[rows, 768:] = (taps[1].astype(F32) + taps[2].astype(F32)).astype(BF)
+        g3[lower, :768] = (taps[0].astype(F32) + taps[1].astype(F32)).astype(BF)
+        g3[lower, 768:] = taps[2]
+        return carry
+
+    lax.fori_loop(0, 12, sum_taps, 0)
+
+    arrive(x2[2:4])
+
+    @pl.when(gy == 0)
+    def _():
+        p1[0, pl.ds(3, 4)] = jnp.zeros((4, 64, 128), BF)
+
+    @pl.when(gy == ny - 1)
+    def _():
+        p1[2, pl.ds(3, 4)] = jnp.zeros((4, 64, 128), BF)
+
+    passed = []
+    for n, dy in enumerate((-1, 1)):
+        passed.append(
+            send(n, mate, 0, p1.at[1 - dy, pl.ds(4 - odd, 3)], p1.at[1 - dy, pl.ds(7 * odd, 3)], sp, rp)
+        )
+    start(passed)
+
+    low = iota((64, 128), 1) < 64
+    e2 = [[None] * 8, [None] * 8]
+
+    def enc2(xs):
+        for g in range(2):
+            lhs = cat(
+                [cat([cat([p1[g, x + i], p1[g + 1, x + i]], 1) for i in range(3)], 1) for x in xs], 0
+            )
+            t = nn(lhs, k2[...])
+            t = gelu(t[:, 256:512] + shifted(t[:, :256], 1, 0, 64) + shifted(t[:, 512:], -1, 0, 64))
+            for n, x in enumerate(xs):
+                v = t[64 * n : 64 * n + 64]
+                halves = [v[:, :128], v[:, 128:]]
+                for h in range(2):
+                    ok = True if h != g else (gy > 0) if g == 0 else (gy < ny - 1)
+                    if x < 2:
+                        ok = ok & (gx > 0)
+                    if x > 5:
+                        ok = ok & (gx < nx - 1)
+                    if ok is not True:
+                        halves[h] = jnp.where(ok, halves[h], jnp.zeros_like(halves[h]))
+                e2[g][x] = [v.astype(BF) for v in halves]
+
+    enc2((3, 4))
+    arrive(x2[:2])
+    arrive(x2[4:])
+    for n, dy in enumerate((-1, 1)):
+        send(n, mate, 0, p1.at[1 - dy, pl.ds(3 + odd, 3)], p1.at[1 - dy, pl.ds(7 - 7 * odd, 3)], sp, rp).wait_recv()
 
     @pl.when(gx == 0)
     def _():
@@ -281,37 +356,19 @@
 
     @pl.when(gy == 0)
     def _():
-        p1[0] = jnp.zeros((10, 64, 128), BF)
+        for x in (0, 7):
+            p1[0, pl.ds(x, 3)] = jnp.zeros((3, 64, 128), BF)
 
     @pl.when(gy == ny - 1)
     def _():
-        p1[2] = jnp.zeros((10, 64, 128), BF)
-
-    low = iota((64, 128), 1) < 64
-    e2 = []
+        for x in (0, 7):
+            p1[2, pl.ds(x, 3)] = jnp.zeros((3, 64, 128), BF)
+
+    enc2((0, 1, 2, 5, 6, 7))
     pairs = []
     for g in range(2):
-        lhs = cat(
-            [cat([cat([p1[g, x + i], p1[g + 1, x + i]], 1) for i in range(3)], 1) for x in range(8)], 0
-        )
-        t = nn(lhs, k2[...])
-        t = gelu(t[:, 256:512] + shifted(t[:, :256], 1, 0, 64) + shifted(t[:, 512:], -1, 0, 64))
-        rows = []
-        for x in range(8):
-            v = t[64 * x : 64 * x + 64]
-            halves = [v[:, :128], v[:, 128:]]
-            for h in range(2):
-                ok = True if h != g else (gy > 0) if g == 0 else (gy < ny - 1)
-                if x < 2:
-                    ok = ok & (gx > 0)
-                if x > 5:
-                    ok = ok & (gx < nx - 1)
-                if ok is not True:
-                    halves[h] = jnp.where(ok, halves[h], jnp.zeros_like(halves[h]))
-            rows.append([v.astype(BF) for v in halves])
-        e2.append(rows)
         for x in range(4):
-            a0, a1 = [rows[2 * x][h].astype(F32) + rows[2 * x + 1][h].astype(F32) for h in range(2)]
+            a0, a1 = [e2[g][2 * x][h].astype(F32) + e2[g][2 * x + 1][h].astype(F32) for h in range(2)]
             a = jnp.where(low, a0 + pltpu.roll(a0, 64, 1), a1 + pltpu.roll(a1, 64, 1))
             pairs.append(((a + pltpu.roll(a, 63, 0)) * 0.125).astype(BF))
     pick32 = ones_where(iota((32, 64), 1) == 2 * iota((32, 64), 0))
@@ -385,11 +442,8 @@
         ],
         0,
     )
-    t = nt(k4[...], lhs)
-    e4 = gelu(t[256:512] + shifted(t[:256], 1, 1, 16) + shifted(t[512:], -1, 1, 16))
-    n = iota((256, 144), 1) // 16
-    x, y = gx - 1 + n // 3, gy - 1 + n % 3
-    e4 = jnp.where((x >= 0) & (x < nx) & (y >= 0) & (y < ny), e4, 0.0).astype(BF)
+    t = nt(lhs, k4[...])
+    e4 = gelu(t[:, 256:512] + shifted(t[:, :256], 1, 0, 16) + shifted(t[:, 512:], -1, 0, 16))
 
     def inside(x, y, width, n_local):
         ok = True
@@ -407,24 +461,26 @@
         return v if ok is True else jnp.where(ok, v, jnp.zeros_like(v))
 
 
-    for c in got_v3:
-        c.wait()
-    up = nt(ones_where(iota((288, 144), 1) == iota((288, 144), 0) // 2), e4).astype(BF)
+    e4 = [kept(e4[16 * n : 16 * n + 16], inside(n // 3, n % 3, 16, 1)).astype(BF) for n in range(9)]
+    twice = ones_where(iota((32, 16), 1) == iota((32, 16), 0) // 2)
+    up = nn(twice, cat(e4, 1)).astype(BF)
     at = ((0, 0, 1), (0, 1, 1), (1, 1, 2), (1, 2, 2))
-    for x in range(4):
+    for k in range(2):
         for y in range(4):
-            for i in range(3):
+            for tx in range(2):
                 for j in range(3):
-                    n = 3 * at[x][i] + at[y][j]
-                    pd3[pl.ds(128 * x + 32 * y, 32), pl.ds(256 * (3 * i + j), 256)] = up[32 * n : 32 * n + 32]
-    t = nt(pd3[...], kd3[...])
-    v = gelu(t[:, 128:256] + shifted(t[:, :128], 1, 0, 32) + shifted(t[:, 256:], -1, 0, 32))
+                    n = 3 * (k + tx) + at[y][j]
+                    pd3[pl.ds(128 * k + 32 * y, 32), pl.ds(256 * (3 * tx + j), 256)] = up[:, 256 * n : 256 * n + 256]
+    t = nt(pd3[...], g3[...])
     arrive(xe3)
-    for x in range(4):
-        for y in range(4):
-            n = 128 * x + 32 * y
-            w = v[n : n + 32] + e3e[x, y].astype(F32)
-            d3e[x, y] = kept(w, inside(x, y, 32, 2)).astype(BF)
+    for px in range(2):
+        u = t[:, 384 * px : 384 * px + 384]
+        v = gelu(u[:, 128:256] + shifted(u[:, :128], 1, 0, 32) + shifted(u[:, 256:], -1, 0, 32))
+        for k in range(2):
+            for y in range(4):
+                x, n = 2 * k + 1 - px, 128 * k + 32 * y
+                w = v[n : n + 32] + e3e[x, y].astype(F32)
+                d3e[x, y] = kept(w, inside(x, y, 32, 2)).astype(BF)
 
     lane = iota((288, 128), 1) < 64
     lhs = cat(
@@ -451,31 +507,42 @@
     spread = ones_where((rr // 4 == cc % 32) & (rr // 2 % 2 == cc // 32))
     for x in range(6):
         line = []
+        as_is = [d2e[x, m] for m in range(6)]
+        turned = [pltpu.roll(v, 64, 1) for v in as_is]
         for m in range(5):
-            a, b = d2e[x, m], d2e[x, m + 1]
-            top = jnp.where(low32, a, pltpu.roll(b, 64, 1))
-            bottom = jnp.where(low32, pltpu.roll(a, 64, 1), b)
+            top = jnp.where(low32, as_is[m], turned[m + 1])
+            bottom = jnp.where(low32, turned[m], as_is[m + 1])
             line.append(cat([top, bottom], 0).astype(BF))
         a = nn(spread, cat(line, 1)).astype(BF)
         for m in range(5):
             q[x, m] = a[:, 128 * m : 128 * m + 128]
 
-    for k in range(5):
-        for ms in ((0, 1), (2, 3), (4,)):
-            t = nt(g1[...], cat([cat([q[k, m], q[k + 1, m]], 1) for m in ms], 0))
-            for px in range(2):
-                for py in range(2):
-                    for h, m in enumerate(ms):
-                        a, b = k - px, m - py
-                        if not (0 <= a < 4 and 0 <= b < 4):
-                            continue
-                        x, y = 2 * a + px, 2 * b + py
-                        n = 96 * (2 * px + py)
-                        u = t[n : n + 96, 128 * h : 128 * h + 128]
-                        v = gelu(u[32:64] + shifted(u[:32], 1, 1, 128) + shifted(u[64:], -1, 1, 128))
-                        v = v + e1[x, pl.ds(32 * y, 32), :].astype(F32)
-                        out[x, y] = v.astype(BF)
-    for copies in (x1, x2, x4, xe3):
+    both = ((0, 0), (0, 1), (1, 0), (1, 1))
+    groups = []
+    for parities, windows in (
+        ([c for c in both if c[0] == 0], [(0, m) for m in range(5)]),
+        ([c for c in both if c[1] == 0], [(k, 0) for k in range(1, 4)]),
+        (both, [(k, m) for k in range(1, 4) for m in range(1, 4)]),
+        ([c for c in both if c[1] == 1], [(k, 4) for k in range(1, 4)]),
+        ([c for c in both if c[0] == 1], [(4, m) for m in range(5)]),
+    ):
+        for n in range(0, len(windows), 2):
+            groups.append((parities, windows[n : n + 2]))
+    for parities, windows in groups:
+        lhs = cat([g1[pl.ds(96 * (2 * px + py), 96), :] for px, py in parities], 0)
+        t = nt(lhs, cat([cat([q[k, m], q[k + 1, m]], 1) for k, m in windows], 0))
+        for n, (px, py) in enumerate(parities):
+            for h, (k, m) in enumerate(windows):
+                a, b = k - px, m - py
+                if not (0 <= a < 4 and 0 <= b < 4):
+                    continue
+                x, y = 2 * a + px, 2 * b + py
+                u = t[96 * n : 96 * n + 96, 128 * h : 128 * h + 128]
+                v = gelu(u[32:64] + shifted(u[:32], 1, 1, 128) + shifted(u[64:], -1, 1, 128))
+                v = v + e1[x, pl.ds(32 * y, 32), :].astype(F32)
+                out[x, y] = v.astype(BF)
+
+    for copies in (x1, x2, passed, x4, xe3):
         for c in copies:
             c.wait_send()
 
@@ -493,13 +560,13 @@
         (3, 10, 64, 128),
         (5, ny + 4, 16, 128), (6, 6, 32, 128), (4, 4, 32, 128),
         (192, 384), (768, 768), (768, 768), (768, 1152), (384, 2304), (1024, 512), (384, 256),
-        (512, 2304), (4, 4, 32, 128),
+        (256, 1536), (768, 1536), (4, 4, 32, 128),
     ):
         scratch.append(pltpu.VMEM(shape, BF))
     scratch.append(pltpu.VMEM((6, 6, 32, 128), F32))
     scratch.append(pltpu.VMEM((6, 5, 128, 128), BF))
     scratch.append(dma((24,)))
-    for n in (8, 8, far, 8):
+    for n in (8, 6, 2, far, 8):
         scratch += [dma((n,)), dma((n,))]
     decoded = pl.pallas_call(
         kernel,

time: 35 us -> 33.8 us (0.966)
  Pallas kernels: 33.9 us -> 32.7 us
    pallas_call x1, Pallas kernels: 33.9 us -> 32.7 us  [local(): pl.pallas_call(kernel, out_shape=pltpu.VMEM((8, 8, 32, 128), BF), in_spec...]
where the time goes in v5:
time: 33.8 us; the launch traced here: 33.7 us
  Pallas kernels  32.7 us (97%)
  local copies, waits for them, and re-layouts  1 us (3%)
    pallas_call x1, Pallas kernels, local(): pl.pallas_call(kernel, out_shape=pltpu.VMEM((8, 8, 32, 128), BF), in_spec...  32.7 us
    transpose x1, local copies, waits for them, and re-layouts, local(): return jnp.transpose(decoded, (2, 0, 1, 3))  1 us

profile of v5, /device:TPU:1, one launch (start us, length us, event | category | flops | bytes accessed | tf_op | source)
XLA Modules:
  0.0 33.7 jit_solution(531674076685215602)
XLA Ops:
  0.0 32.7 %shard_map.82 = bf16[8,8,32,128]{3,2,1,0:T(8,128)(2,1)S(1)} custom-call(bf16[32,8,8,128]{3,2,1,0:T(8,128)(2,1)} %feat.1, bf16[27,32,32]{2,1,0:T(8,128)(2,1)} %w1h.1, bf16[27,32,64]{2,1,0:T(8,128)(2,1)} %bitcast.9, bf16[27,64,128]{2,1,0:T(8,128)(2,1)} %bitcast.8, bf16[9,768,128]{2,1,0:T(8,128)(2,1)} %bitcast.6, bf16[9,384,256]{2,1,0:T(8,128)(2,1)} %bitcast.7, ...), custom_call_target="tpu_custom_call" | custom-call | flops 2230000128 | bytes 7000000 | tf_op jit(solution)/shard_map/pallas_call | solution.py:571
  32.7 1.0 %copy.9 = bf16[32,8,8,128]{3,2,1,0:T(8,128)(2,1)} copy(bf16[32,8,8,128]{3,0,2,1:T(8,128)(2,1)S(1)} %bitcast.5) | data formatting | bytes 1048576 | tf_op jit(solution)/shard_map/transpose | solution.py:582

commit v6 on v5

--- a/solution.py
+++ b/solution.py
@@ -210,7 +210,21 @@
         return a.astype(BF)
 
     pick64 = ones_where(iota((64, 128), 1) == 2 * iota((64, 128), 0))
-    pooled = [None, pool1(1), pool1(2), None]
+    t = nt(pick64, cat([pool1(1), pool1(2)], 0)).astype(BF)
+    p1[1, 4], p1[1, 5] = t[:, :128], t[:, 128:]
+
+    odd = lax.rem(gx, 2)
+    mate = 1 - 2 * odd
+    inner = p1.at[1, pl.ds(4, 2)]
+    x2 = []
+    for n, dy in enumerate((-1, 1)):
+        x2.append(send(n, -mate, dy, inner, p1.at[1 - dy, pl.ds(8 - 8 * odd, 2)], s2, r2))
+    for n, dy in enumerate((-1, 1)):
+        x2.append(send(2 + n, 0, dy, inner, p1.at[1 - dy, pl.ds(4, 2)], s2, r2))
+    x2.append(send(4, -1, 0, inner, p1.at[1, pl.ds(8, 2)], s2, r2))
+    x2.append(send(5, 1, 0, inner, p1.at[1, pl.ds(0, 2)], s2, r2))
+    start(x2)
+
     arrive(x1[4:6])
 
     @pl.when(gx == 0)
@@ -243,21 +257,16 @@
 
     enc1(0, 7, 0)
     enc1(0, 7, 3)
-    pooled[0], pooled[3] = pool1(0), pool1(3)
-
-    t = nt(pick64, cat(pooled, 0)).astype(BF)
-    for x in range(4):
-        p1[1, x + 3] = t[:, 128 * x : 128 * x + 128]
-    odd = lax.rem(gx, 2)
-    mate = 1 - 2 * odd
-    x2 = []
+    t = nt(pick64, cat([pool1(0), pool1(3)], 0)).astype(BF)
+    p1[1, 3], p1[1, 6] = t[:, :128], t[:, 128:]
+    x2b = []
     for n, dy in enumerate((-1, 1)):
-        x2.append(send(n, -mate, dy, p1.at[1, pl.ds(3 + odd, 3)], p1.at[1 - dy, pl.ds(7 - 7 * odd, 3)], s2, r2))
-    for n, dy in enumerate((-1, 1)):
-        x2.append(send(2 + n, 0, dy, p1.at[1, pl.ds(3, 4)], p1.at[1 - dy, pl.ds(3, 4)], s2, r2))
-    x2.append(send(4, -1, 0, p1.at[1, pl.ds(3, 3)], p1.at[1, pl.ds(7, 3)], s2, r2))
-    x2.append(send(5, 1, 0, p1.at[1, pl.ds(4, 3)], p1.at[1, pl.ds(0, 3)], s2, r2))
-    start(x2)
+        x2b.append(send(6 + n, -mate, dy, p1.at[1, 3 + 3 * odd], p1.at[1 - dy, 7 - 5 * odd], s2, r2))
+    for n, (dy, x) in enumerate(((-1, 3), (1, 3), (-1, 6), (1, 6))):
+        x2b.append(send(8 + n, 0, dy, p1.at[1, x], p1.at[1 - dy, x], s2, r2))
+    x2b.append(send(12, -1, 0, p1.at[1, 3], p1.at[1, 7], s2, r2))
+    x2b.append(send(13, 1, 0, p1.at[1, 6], p1.at[1, 2], s2, r2))
+    start(x2b)
 
     got_v2.wait()
     for px in range(2):
@@ -300,22 +309,28 @@
 
     lax.fori_loop(0, 12, sum_taps, 0)
 
-    arrive(x2[2:4])
-
-    @pl.when(gy == 0)
-    def _():
-        p1[0, pl.ds(3, 4)] = jnp.zeros((4, 64, 128), BF)
-
-    @pl.when(gy == ny - 1)
-    def _():
-        p1[2, pl.ds(3, 4)] = jnp.zeros((4, 64, 128), BF)
-
     passed = []
-    for n, dy in enumerate((-1, 1)):
-        passed.append(
-            send(n, mate, 0, p1.at[1 - dy, pl.ds(4 - odd, 3)], p1.at[1 - dy, pl.ds(7 * odd, 3)], sp, rp)
-        )
-    start(passed)
+    for part, xs in ((x2[2:4], (4, 5)), (x2b[2:6], (3, 6))):
+        arrive(part)
+
+        @pl.when(gy == 0)
+        def _():
+            for x in xs:
+                p1[0, x] = jnp.zeros((64, 128), BF)
+
+        @pl.when(gy == ny - 1)
+        def _():
+            for x in xs:
+                p1[2, x] = jnp.zeros((64, 128), BF)
+
+        new = []
+        for n, y in enumerate((2, 0)):
+            if xs == (4, 5):
+                new.append(send(n, mate, 0, p1.at[y, pl.ds(4, 2)], p1.at[y, pl.ds(8 * odd, 2)], sp, rp))
+            else:
+                new.append(send(2 + n, mate, 0, p1.at[y, 6 - 3 * odd], p1.at[y, 2 + 5 * odd], sp, rp))
+        start(new)
+        passed += new
 
     low = iota((64, 128), 1) < 64
     e2 = [[None] * 8, [None] * 8]
@@ -343,8 +358,11 @@
     enc2((3, 4))
     arrive(x2[:2])
     arrive(x2[4:])
-    for n, dy in enumerate((-1, 1)):
-        send(n, mate, 0, p1.at[1 - dy, pl.ds(3 + odd, 3)], p1.at[1 - dy, pl.ds(7 - 7 * odd, 3)], sp, rp).wait_recv()
+    arrive(x2b[:2])
+    arrive(x2b[6:])
+    for n, y in enumerate((2, 0)):
+        send(n, mate, 0, p1.at[y, pl.ds(4, 2)], p1.at[y, pl.ds(8 - 8 * odd, 2)], sp, rp).wait_recv()
+        send(2 + n, mate, 0, p1.at[y, 3 + 3 * odd], p1.at[y, 7 - 5 * odd], sp, rp).wait_recv()
 
     @pl.when(gx == 0)
     def _():
@@ -542,7 +560,7 @@
                 v = v + e1[x, pl.ds(32 * y, 32), :].astype(F32)
                 out[x, y] = v.astype(BF)
 
-    for copies in (x1, x2, passed, x4, xe3):
+    for copies in (x1, x2, x2b, passed, x4, xe3):
         for c in copies:
             c.wait_send()
 
@@ -566,7 +584,7 @@
     scratch.append(pltpu.VMEM((6, 6, 32, 128), F32))
     scratch.append(pltpu.VMEM((6, 5, 128, 128), BF))
     scratch.append(dma((24,)))
-    for n in (8, 6, 2, far, 8):
+    for n in (8, 14, 4, far, 8):
         scratch += [dma((n,)), dma((n,))]
     decoded = pl.pallas_call(
         kernel,

time: 33.8 us -> 33.3 us (0.985)
  Pallas kernels: 32.7 us -> 32.2 us
    pallas_call x1, Pallas kernels: 32.7 us -> 32.2 us  [local(): pl.pallas_call(kernel, out_shape=pltpu.VMEM((8, 8, 32, 128), BF), in_spec...]
where the time goes in v6:
time: 33.3 us; the launch traced here: 33.2 us
  Pallas kernels  32.2 us (97%)
  local copies, waits for them, and re-layouts  1 us (3%)
    pallas_call x1, Pallas kernels, local(): pl.pallas_call(kernel, out_shape=pltpu.VMEM((8, 8, 32, 128), BF), in_spec...  32.2 us
    transpose x1, local copies, waits for them, and re-layouts, local(): return jnp.transpose(decoded, (2, 0, 1, 3))  1 us

profile of v6, /device:TPU:1, one launch (start us, length us, event | category | flops | bytes accessed | tf_op | source)
XLA Modules:
  0.0 33.2 jit_solution(17108038788485779811)
XLA Ops:
  0.0 32.2 %shard_map.82 = bf16[8,8,32,128]{3,2,1,0:T(8,128)(2,1)S(1)} custom-call(bf16[32,8,8,128]{3,2,1,0:T(8,128)(2,1)} %feat.1, bf16[27,32,32]{2,1,0:T(8,128)(2,1)} %w1h.1, bf16[27,32,64]{2,1,0:T(8,128)(2,1)} %bitcast.9, bf16[27,64,128]{2,1,0:T(8,128)(2,1)} %bitcast.8, bf16[9,768,128]{2,1,0:T(8,128)(2,1)} %bitcast.6, bf16[9,384,256]{2,1,0:T(8,128)(2,1)} %bitcast.7, ...), custom_call_target="tpu_custom_call" | custom-call | flops 2230000128 | bytes 7000000 | tf_op jit(solution)/shard_map/pallas_call | solution.py:589
  32.2 1.0 %copy.9 = bf16[32,8,8,128]{3,2,1,0:T(8,128)(2,1)} copy(bf16[32,8,8,128]{3,0,2,1:T(8,128)(2,1)S(1)} %bitcast.5) | data formatting | bytes 1048576 | tf_op jit(solution)/shard_map/transpose | solution.py:600

commit v7 on v6

--- a/solution.py
+++ b/solution.py
@@ -76,9 +76,9 @@
         return (lax.rem(gx + dx + nx, nx), lax.rem(gy + dy + ny, ny))
 
     barrier = pltpu.get_barrier_semaphore()
-    got_feat = load(feat, fv)
     for dx, dy in DIRS:
         pl.semaphore_signal(barrier, inc=1, device_id=target(dx, dy), device_id_type=MESH)
+    got_feat = load(feat, fv)
     got_w1, got_w2, got_w3 = load(w1h, w1), load(w2h, w2), load(w3h, w3)
     got_v2, got_v1 = load(v2h, v2), load(v1h, v1)
     got_w4 = [load(w4h.at[n], k4.at[:, pl.ds(128 * n, 128)]) for n in range(9)]
@@ -128,7 +128,9 @@
         x1.append(
             send(n, dx, dy, fext.at[pl.ds(sx, cx), pl.ds(sy, cy)], fext.at[pl.ds(tx, cx), pl.ds(ty, cy)], s1, r1)
         )
-    start(x1)
+    start(x1[:4])
+    start(x1[6:])
+    start(x1[4:6])
 
     got_w1.wait()
     t = None
@@ -201,7 +203,8 @@
     def _():
         fext[pl.ds(1, 8), pl.ds(288, 32)] = jnp.zeros((8, 32, 128), BF)
 
-    lax.fori_loop(0, 3, functools.partial(enc1_inner, blocks=(0, 3)), 0)
+    for n in range(3):
+        enc1_inner(n, 0, (0, 3))
 
     def pool1(x):
         a = e1[2 * x].astype(F32) + e1[2 * x + 1].astype(F32)

time: 33.3 us -> 33.1 us (level)
  no operation moved by 1% of the time
where the time goes in v7:
time: 33.1 us; the launch traced here: 33 us
  Pallas kernels  32 us (97%)
  local copies, waits for them, and re-layouts  1 us (3%)
    pallas_call x1, Pallas kernels, local(): pl.pallas_call(kernel, out_shape=pltpu.VMEM((8, 8, 32, 128), BF), in_spec...  32 us
    transpose x1, local copies, waits for them, and re-layouts, local(): return jnp.transpose(decoded, (2, 0, 1, 3))  1 us

profile of v7, /device:TPU:1, one launch (start us, length us, event | category | flops | bytes accessed | tf_op | source)
XLA Modules:
  0.0 33.0 jit_solution(1403637480341313667)
XLA Ops:
  0.0 32.0 %shard_map.82 = bf16[8,8,32,128]{3,2,1,0:T(8,128)(2,1)S(1)} custom-call(bf16[32,8,8,128]{3,2,1,0:T(8,128)(2,1)} %feat.1, bf16[27,32,32]{2,1,0:T(8,128)(2,1)} %w1h.1, bf16[27,32,64]{2,1,0:T(8,128)(2,1)} %bitcast.9, bf16[27,64,128]{2,1,0:T(8,128)(2,1)} %bitcast.8, bf16[9,768,128]{2,1,0:T(8,128)(2,1)} %bitcast.6, bf16[9,384,256]{2,1,0:T(8,128)(2,1)} %bitcast.7, ...), custom_call_target="tpu_custom_call" | custom-call | flops 2230000128 | bytes 7000000 | tf_op jit(solution)/shard_map/pallas_call | solution.py:592
  32.0 1.0 %copy.9 = bf16[32,8,8,128]{3,2,1,0:T(8,128)(2,1)} copy(bf16[32,8,8,128]{3,0,2,1:T(8,128)(2,1)S(1)} %bitcast.5) | data formatting | bytes 1048576 | tf_op jit(solution)/shard_map/transpose | solution.py:603

commit v8 on v7

--- a/solution.py
+++ b/solution.py
@@ -385,7 +385,8 @@
         for x in (0, 7):
             p1[2, pl.ds(x, 3)] = jnp.zeros((3, 64, 128), BF)
 
-    enc2((0, 1, 2, 5, 6, 7))
+    enc2((0, 1, 2))
+    enc2((5, 6, 7))
     pairs = []
     for g in range(2):
         for x in range(4):

time: 33.1 us -> 33.1 us (level)
  no operation moved by 1% of the time
where the time goes in v8:
time: 33.1 us; the launch traced here: 33 us
  Pallas kernels  31.9 us (96%)
  local copies, waits for them, and re-layouts  1 us (3%)
    pallas_call x1, Pallas kernels, local(): pl.pallas_call(kernel, out_shape=pltpu.VMEM((8, 8, 32, 128), BF), in_spec...  31.9 us
    transpose x1, local copies, waits for them, and re-layouts, local(): return jnp.transpose(decoded, (2, 0, 1, 3))  1 us

profile of v8, /device:TPU:1, one launch (start us, length us, event | category | flops | bytes accessed | tf_op | source)
XLA Modules:
  0.0 33.0 jit_solution(1551526626489832971)
XLA Ops:
  0.0 31.9 %shard_map.82 = bf16[8,8,32,128]{3,2,1,0:T(8,128)(2,1)S(1)} custom-call(bf16[32,8,8,128]{3,2,1,0:T(8,128)(2,1)} %feat.1, bf16[27,32,32]{2,1,0:T(8,128)(2,1)} %w1h.1, bf16[27,32,64]{2,1,0:T(8,128)(2,1)} %bitcast.9, bf16[27,64,128]{2,1,0:T(8,128)(2,1)} %bitcast.8, bf16[9,768,128]{2,1,0:T(8,128)(2,1)} %bitcast.6, bf16[9,384,256]{2,1,0:T(8,128)(2,1)} %bitcast.7, ...), custom_call_target="tpu_custom_call" | custom-call | flops 2230000128 | bytes 7000000 | tf_op jit(solution)/shard_map/pallas_call | solution.py:593
  32.0 1.0 %copy.9 = bf16[32,8,8,128]{3,2,1,0:T(8,128)(2,1)} copy(bf16[32,8,8,128]{3,0,2,1:T(8,128)(2,1)S(1)} %bitcast.5) | data formatting | bytes 1048576 | tf_op jit(solution)/shard_map/transpose | solution.py:604
